TPU v7x, 256 devices: a whole 4x4x8 slice. The times are simulated.
256 devices in a mesh: head: 8 (over y, core), ctx: 32 (over z, x).
Axes of the slice: x: 4, y: 4, z: 8, core: 2. Of those that a mesh axis runs over, the one named last changes fastest.
Arguments:
- queries: bfloat16 [65536, 4096], P('ctx', 'head'), may hold values from -6 to 6
- keys: bfloat16 [65536, 4096], P('ctx', 'head'), may hold values from -6 to 6
- values: bfloat16 [65536, 4096], P('ctx', 'head'), may hold values from -23 to 23
- level_table: float32 [4, 9], replicated, may hold values from 0.3 to 3
- head_table: int32 [32], replicated, may hold values from 0 to 3
- gain: float32 [4096], P('head'), may hold values from 0.5 to 1.5
Outputs:
- attended: bfloat16 [65536, 4096], P('ctx', 'head')
All inputs are finite; a program needn't handle non-finite values.
Results may differ from a plain program's by a relative error of at most 0.0043.
Values sent between devices are 32-bit elements; how exact they have to be, the bound alone decides.
A program may use at most 192 MiB of HBM per device.

v0:
```python
import jax
import jax.numpy as jnp
from jax import lax
from jax.sharding import PartitionSpec as P

HEAD_DIM = 128
LEAF = 256
PROFILES = 4
LEAVES_SEG = 8
D = 4096


epsilon = 1e-06


def partner(value, axis, apart):
    return lax.ppermute(value, axis, [(i, i ^ 1 << apart) for i in range(lax.axis_size(axis))])


def copy_for_each(value, axis):
    length = lax.axis_size(axis)
    return lax.all_to_all(
        jnp.broadcast_to(value[None], (length, *value.shape)), axis, 0, 0, tiled=True
    )


def taken_together(value, axis):
    everything = copy_for_each(value, axis)
    return jnp.sum(everything, axis=0)


def level_scales(level_count):
    level_ids = jnp.arange(level_count, dtype=jnp.int32)
    bucket_sizes = jnp.exp2(jnp.maximum(level_ids - 1, 0).astype(jnp.float32)) * jnp.float32(LEAF)
    return 1.0 / jnp.sqrt(bucket_sizes)


def tile_levels(query_pos, key_pos, local_bits):
    distance = jnp.bitwise_xor((query_pos // LEAF)[:, None], (key_pos // LEAF)[None, :])
    level_ids = jnp.zeros(distance.shape, jnp.int32)
    for level_bit in range(local_bits):
        level_ids = level_ids + (distance >= 1 << level_bit).astype(jnp.int32)
    return level_ids


def tile_weights(query_pos, key_pos, effective, local_bits):
    level_ids = tile_levels(query_pos, key_pos, local_bits)
    weight = jnp.zeros((effective.shape[0],) + level_ids.shape, effective.dtype)
    for level_num in range(local_bits + 1):
        member = jnp.where(level_ids == level_num, 1.0, 0.0).astype(effective.dtype)
        weight = weight + member[None] * effective[:, level_num, None, None]
    causal = key_pos[None, :] <= query_pos[:, None]
    return jnp.where(causal[None], weight, 0.0)


def shards(queries, keys, values, level_table, head_table, gain):
    seg_length = queries.shape[0]
    heads_here = queries.shape[1] // HEAD_DIM
    local_bits = LEAVES_SEG.bit_length() - 1
    ctx_bits = lax.axis_size("ctx").bit_length() - 1
    selector = (head_table[:, None] == jnp.arange(PROFILES, dtype=jnp.int32)[None, :]).astype(
        jnp.float32
    )
    chosen = jnp.dot(selector, level_table, precision=lax.Precision.HIGHEST)
    mine = lax.dynamic_slice_in_dim(chosen, lax.axis_index("head") * heads_here, heads_here, 0)
    effective = mine * level_scales(level_table.shape[1])[None, :]
    query_rows = queries.reshape(seg_length, heads_here, HEAD_DIM)
    key_rows = keys.reshape(seg_length, heads_here, HEAD_DIM)
    value_rows = values.reshape(seg_length, heads_here, HEAD_DIM)
    own_state = jnp.einsum("thd,the->hde", key_rows, value_rows, preferred_element_type=jnp.float32)
    segment = lax.axis_index("ctx")
    block_sum = own_state
    distant = jnp.zeros_like(own_state)
    for level_bit in range(ctx_bits):
        sibling = partner(block_sum, "ctx", level_bit)
        member = (segment >> level_bit & 1).astype(jnp.float32)
        factor = member * effective[:, local_bits + 1 + level_bit]
        distant = distant + factor[:, None, None] * sibling
        block_sum = block_sum + sibling
    block_rows = min(512, seg_length)
    block_count = seg_length // block_rows
    pieces = []
    for block_num in range(block_count):
        first = block_num * block_rows
        reach = first + block_rows
        query_block = query_rows[first:reach]
        key_span = key_rows[:reach]
        value_span = value_rows[:reach]
        query_pos = first + jnp.arange(block_rows, dtype=jnp.int32)
        key_pos = jnp.arange(reach, dtype=jnp.int32)
        scores = jnp.einsum(
            "thd,shd->hts", query_block, key_span, preferred_element_type=jnp.float32
        )
        weight = tile_weights(query_pos, key_pos, effective, local_bits)
        rounded = (scores * weight).astype(jnp.bfloat16)
        pieces.append(
            jnp.einsum("hts,shd->thd", rounded, value_span, preferred_element_type=jnp.float32)
        )
    nearby = jnp.concatenate(pieces, axis=0)
    remote = jnp.einsum(
        "thd,hde->the", query_rows.astype(jnp.float32), distant, precision=lax.Precision.HIGHEST
    )
    combined = (nearby + remote).reshape(seg_length, heads_here * HEAD_DIM)
    squares = taken_together(jnp.sum(combined * combined, axis=1), "head")
    inverse = lax.rsqrt(squares / D + epsilon)
    return (combined * inverse[:, None] * gain[None, :]).astype(jnp.bfloat16)


def solution(mesh):
    return jax.shard_map(
        shards,
        mesh=mesh,
        in_specs=(P("ctx", "head"), P("ctx", "head"), P("ctx", "head"), P(), P(), P("head")),
        out_specs=P("ctx", "head"),
        check_vma=False,
    )
```

profile of v0, /device:TPU:1, one launch (start us, length us, event | category | flops | bytes accessed | tf_op | source)
XLA Modules:
  0.0 152.2 jit_solution(273175382784850049)
XLA Ops:
  0.0 4.1 %copy.124 = bf16[2048,512]{0,1:T(8,128)(2,1)} copy(bf16[2048,512]{1,0:T(8,128)(2,1)} %param.7) | data formatting | bytes 4194304 | tf_op jit(solution)/shard_map/reshape | solution.py:68
  4.1 2.3 %fusion.26 = f32[4,128,128]{2,1,0:T(8,128)S(1)} fusion(bf16[2048,4,128]{0,2,1:T(8,128)(2,1)} %bitcast.63, bf16[2048,512]{1,0:T(8,128)(2,1)S(1)} %copy-done.2), kind=kOutput, calls=%fused_computation.44 | convolution fusion | flops 268435456 | bytes 4456448 | tf_op jit(solution)/shard_map/thd,the->hde/dot_general | solution.py:70
  6.4 2.1 %collective-permute-start = (f32[4,128,128]{2,1,0:T(8,128)S(1)}, f32[4,128,128]{2,1,0:T(8,128)}, u32[]{:S(2)}, u32[]{:S(2)}) collective-permute-start(f32[4,128,128]{2,1,0:T(8,128)S(1)} %fusion.26), channel_id=1, source_target_pairs={{0,1},{1,0},{2,3},{3,2},{4,5},{5,4},{6,7},{7,6},{8,9},{9,8},{10,11... | collective-permute-start | bytes 786440 | tf_op jit(solution)/shard_map/ppermute | solution.py:17
  8.7 3.0 %fusion.96 = (bf16[512,512]{1,0:T(8,128)(2,1)}, bf16[512,512]{1,0:T(8,128)(2,1)}, bf16[512,512]{1,0:T(8,128)(2,1)}, bf16[512,512]{1,0:T(8,128)(2,1)}) fusion(bf16[2048,512]{1,0:T(8,128)(2,1)} %param.6), kind=kLoop, calls=%fused_computation.166 | loop fusion | bytes 4194304 | tf_op jit(solution)/shard_map/slice | solution.py:86
  11.7 2.0 %copy.120 = bf16[512,512]{0,1:T(8,128)(2,1)} copy(bf16[512,512]{1,0:T(8,128)(2,1)} %get-tuple-element.15) | data formatting | bytes 1048576
  13.8 1.6 %copy.122 = bf16[1536,512]{0,1:T(8,128)(2,1)} copy(bf16[1536,512]{1,0:T(8,128)(2,1)S(1)} %slice-done.3) | data formatting | bytes 3145728
  15.4 1.6 %copy.121 = bf16[1536,512]{0,1:T(8,128)(2,1)} copy(bf16[1536,512]{1,0:T(8,128)(2,1)S(1)} %slice-done) | data formatting | bytes 3145728
  17.0 1.4 iota_compare_fusion.1
  20.3 6.1 %fusion.20 = (f32[512,1536]{1,0:T(8,128)}, f32[512,1536]{1,0:T(8,128)}, f32[512,1536]{1,0:T(8,128)}, f32[512,1536]{1,0:T(8,128)}) fusion(s32[1536]{0:T(1024)S(1)} %add_select_fusion.1, s32[512]{0:T(512)S(1)} %add_select_fusion.4), kind=kLoop, calls=%fused_computation.38 | loop fusion | flops 13369344 | bytes 12591104 | tf_op jit(solution)/shard_map/jit(_where)/select_n | solution.py:50
  26.4 6.7 %fusion.9 = (f32[512,2048]{1,0:T(8,128)}, f32[512,2048]{1,0:T(8,128)}, f32[512,2048]{1,0:T(8,128)}, f32[512,2048]{1,0:T(8,128)}) fusion(s32[2048]{0:T(1024)S(1)} %add_select_fusion, s32[512]{0:T(512)S(1)} %add_select_fusion.3), kind=kLoop, calls=%fused_computation.23 | loop fusion | flops 17825792 | bytes 16787456 | tf_op jit(solution)/shard_map/jit(_where)/select_n | solution.py:50
  33.5 15.6 %fusion.44 = f32[512,4,128]{2,0,1:T(8,128)} fusion(f32[4]{0:T(128)S(1)} %get-tuple-element.10, f32[512,2048]{1,0:T(8,128)} %get-tuple-element.24, f32[4]{0:T(128)S(1)} %get-tuple-element.11, f32[512,2048]{1,0:T(8,128)} %get-tuple-element.23, f32[4]{0:T(128)S(1)} %get-tuple-element.12, f32[512,2048]{1,0:T(8,128)} %get-tuple-element.25, ...), kind=kOutput, calls=%fused_computation.67 | convolution fusion | flops 2189426688 | bytes 23593024 | tf_op jit(solution)/shard_map/hts,shd->thd/dot_general | solution.py:97
  49.1 12.6 %fusion.41 = f32[512,4,128]{2,0,1:T(8,128)} fusion(bf16[1536,4,128]{0,2,1:T(8,128)(2,1)} %bitcast.65, bf16[512,4,128]{0,2,1:T(8,128)(2,1)} %bitcast.69, bf16[1536,4,128]{0,2,1:T(8,128)(2,1)} %bitcast.66, f32[4]{0:T(128)S(1)} %get-tuple-element.10, f32[512,1536]{1,0:T(8,128)} %get-tuple-element.20, f32[4]{0:T(128)S(1)} %get-tuple-element.11, ...), kind=kOutput, calls=%fused_computation.64 | convolution fusion | flops 1642070016 | bytes 18088000 | tf_op jit(solution)/shard_map/hts,shd->thd/dot_general | solution.py:97
  61.7 4.3 %fusion.33 = (f32[512,1024]{1,0:T(8,128)}, f32[512,1024]{1,0:T(8,128)}, f32[512,1024]{1,0:T(8,128)}, f32[512,1024]{1,0:T(8,128)}) fusion(s32[1024]{0:T(1024)S(1)} %add_select_fusion.2, s32[512]{0:T(512)S(1)} %add_select_fusion.5), kind=kLoop, calls=%fused_computation.53 | loop fusion | flops 8912896 | bytes 8394752 | tf_op jit(solution)/shard_map/jit(_where)/select_n | solution.py:50
  66.1 1.1 add.386
  67.2 2.5 %collective-permute-start.1 = (f32[4,128,128]{2,1,0:T(8,128)S(1)}, f32[4,128,128]{2,1,0:T(8,128)}, u32[]{:S(2)}, u32[]{:S(2)}) collective-permute-start(f32[4,128,128]{2,1,0:T(8,128)S(1)} %add.386), channel_id=1, source_target_pairs={{0,2},{1,3},{2,0},{3,1},{4,6},{5,7},{6,4},{7,5},{8,10},{9,11},{10,... | collective-permute-start | bytes 786440 | tf_op jit(solution)/shard_map/ppermute | solution.py:17
  70.8 2.1 %copy.117 = bf16[512,512]{0,1:T(8,128)(2,1)} copy(bf16[512,512]{1,0:T(8,128)(2,1)} %get-tuple-element.16) | data formatting | bytes 1048576
  72.8 1.3 copy.118
  74.1 2.3 %copy.119 = bf16[1024,512]{0,1:T(8,128)(2,1)} copy(bf16[1024,512]{1,0:T(8,128)(2,1)} %slice.113) | data formatting | bytes 2097152
  77.9 1.7 %collective-permute-start.2 = (f32[4,128,128]{2,1,0:T(8,128)S(1)}, f32[4,128,128]{2,1,0:T(8,128)}, u32[]{:S(2)}, u32[]{:S(2)}) collective-permute-start(f32[4,128,128]{2,1,0:T(8,128)S(1)} %add.388), channel_id=1, source_target_pairs={{0,4},{1,5},{2,6},{3,7},{4,0},{5,1},{6,2},{7,3},{8,12},{9,13},{10,... | collective-permute-start | bytes 786440 | tf_op jit(solution)/shard_map/ppermute | solution.py:17
  79.6 9.6 %fusion.43 = f32[512,4,128]{2,0,1:T(8,128)} fusion(bf16[1024,4,128]{0,2,1:T(8,128)(2,1)} %bitcast.68, f32[4]{0:T(128)S(1)} %get-tuple-element.10, f32[512,1024]{1,0:T(8,128)} %get-tuple-element.28, f32[4]{0:T(128)S(1)} %get-tuple-element.11, f32[512,1024]{1,0:T(8,128)} %get-tuple-element.27, f32[4]{0:T(128)S(1)} %get-tuple-element.12, ...), kind=kOutput, calls=%fused_computation.66 | convolution fusion | flops 1094713344 | bytes 12582976 | tf_op jit(solution)/shard_map/hts,shd->thd/dot_general | solution.py:97
  89.2 2.1 %copy.114 = bf16[512,512]{0,1:T(8,128)(2,1)} copy(bf16[512,512]{1,0:T(8,128)(2,1)} %get-tuple-element.14) | data formatting | bytes 1048576
  95.1 3.1 %collective-permute-start.3 = (f32[4,128,128]{2,1,0:T(8,128)S(1)}, f32[4,128,128]{2,1,0:T(8,128)S(1)}, u32[]{:S(2)}, u32[]{:S(2)}) collective-permute-start(f32[4,128,128]{2,1,0:T(8,128)S(1)} %add.390), channel_id=1, source_target_pairs={{0,8},{1,9},{2,10},{3,11},{4,12},{5,13},{6,14},{7,15},{8,0},{9,1},... | collective-permute-start | bytes 786440 | tf_op jit(solution)/shard_map/ppermute | solution.py:17
  98.2 2.3 %fusion.51 = (f32[512,512]{1,0:T(8,128)S(1)}, f32[512,512]{1,0:T(8,128)}, f32[512,512]{1,0:T(8,128)}, f32[512,512]{1,0:T(8,128)}) fusion(s32[512]{0:T(512)S(1)} %add_select_fusion.6), kind=kLoop, calls=%fused_computation.74 | loop fusion | flops 4456448 | bytes 4196352 | tf_op jit(solution)/shard_map/jit(_where)/select_n | solution.py:50
  100.5 9.8 %collective-permute-done.3 = f32[4,128,128]{2,1,0:T(8,128)S(1)} collective-permute-done((f32[4,128,128]{2,1,0:T(8,128)S(1)}, f32[4,128,128]{2,1,0:T(8,128)S(1)}, u32[]{:S(2)}, u32[]{:S(2)}) %collective-permute-start.3) | collective-permute-done | bytes 262176 | tf_op jit(solution)/shard_map/ppermute | solution.py:17
  111.1 5.1 %collective-permute-start.4 = (f32[4,128,128]{2,1,0:T(8,128)}, f32[4,128,128]{2,1,0:T(8,128)}, u32[]{:S(2)}, u32[]{:S(2)}) collective-permute-start(f32[4,128,128]{2,1,0:T(8,128)} %add.392), channel_id=1, source_target_pairs={{0,16},{1,17},{2,18},{3,19},{4,20},{5,21},{6,22},{7,23},{8,24},{9,... | collective-permute-start | bytes 786440 | tf_op jit(solution)/shard_map/ppermute | solution.py:17
  116.2 6.0 %fusion.42 = f32[512,4,128]{2,0,1:T(8,128)} fusion(bf16[512,4,128]{0,2,1:T(8,128)(2,1)} %bitcast.73, bf16[512,4,128]{0,2,1:T(8,128)(2,1)} %bitcast.71, bf16[512,4,128]{0,2,1:T(8,128)(2,1)} %bitcast.72, f32[4]{0:T(128)S(1)} %get-tuple-element.10, f32[512,512]{1,0:T(8,128)} %get-tuple-element.31, f32[4]{0:T(128)S(1)} %get-tuple-element.11, ...), kind=kOutput, calls=%fused_computation.65 | convolution fusion | flops 547356672 | bytes 7077952 | tf_op jit(solution)/shard_map/hts,shd->thd/dot_general | solution.py:97
  122.1 6.2 %collective-permute-done.4 = f32[4,128,128]{2,1,0:T(8,128)} collective-permute-done((f32[4,128,128]{2,1,0:T(8,128)}, f32[4,128,128]{2,1,0:T(8,128)}, u32[]{:S(2)}, u32[]{:S(2)}) %collective-permute-start.4) | collective-permute-done | bytes 262176 | tf_op jit(solution)/shard_map/ppermute | solution.py:17
  128.3 6.7 %multiply_reduce_fusion = (f32[2048]{0:T(1024)S(1)}, f32[2048,4,128]{2,0,1:T(8,128)}) fusion(f32[4,128,128]{2,1,0:T(8,128)} %collective-permute-done.4, f32[4,128,128]{2,1,0:T(8,128)S(1)} %collective-permute-done.3, f32[4,128,128]{2,1,0:T(8,128)} %collective-permute-done.2, f32[4,128,128]{2,1,0:T(8,128)} %collective-permute-done.1, ...), kind=kOutput, calls=%fused_computation.15 | convolution fusion | flops 1617491968 | bytes 11804752 | tf_op jit(solution)/shard_map/thd,hde->the/dot_general | solution.py:100
  135.7 5.8 %all-to-all-start = ((f32[8,1,2048]{2,1,0:T(1,128)}), f32[8,1,2048]{2,1,0:T(1,128)S(1)}, u32[]{:S(2)}, u32[]{:S(2)}) async-start(f32[8,1,2048]{2,1,0:T(1,128)} %broadcast_in_dim.172), calls=%async_computation | async-start | bytes 131072 | tf_op jit(solution)/shard_map/all_to_all | solution.py:22
  141.5 5.5 %copy.98 = f32[2048,4,128]{0,2,1:T(8,128)} copy(f32[2048,4,128]{2,0,1:T(8,128)} %get-tuple-element.35) | data formatting | bytes 8388608 | tf_op jit(solution)/shard_map/add | solution.py:103
  147.1 2.6 %fusion.4 = bf16[2048,512]{0,1:T(8,128)(2,1)S(1)} fusion(f32[2048,4,128]{0,2,1:T(8,128)} %copy.98, f32[512]{0:T(512)S(1)} %copy-done.9, f32[2048]{0:T(1024)S(1)} %add_rsqrt_fusion), kind=kLoop, calls=%fused_computation.14 | loop fusion | flops 3145728 | bytes 6301696 | tf_op jit(solution)/shard_map/convert_element_type | solution.py:106
  149.7 2.5 %copy.100 = bf16[2048,512]{1,0:T(8,128)(2,1)} copy(bf16[2048,512]{0,1:T(8,128)(2,1)S(1)} %fusion.4) | data formatting | bytes 4194304 | tf_op jit(solution)/shard_map/convert_element_type | solution.py:106
  (63 shorter events, 10.1 us)
Async XLA Ops:
  0.0 20.1 %copy-start = (f32[4,9]{1,0:T(4,128)S(1)}, f32[4,9]{1,0:T(4,128)}, u32[]{:S(2)}) copy-start(f32[4,9]{1,0:T(4,128)} %param.9) | copy-start | bytes 436
  0.0 4.1 %copy-start.2 = (bf16[2048,512]{1,0:T(8,128)(2,1)S(1)}, bf16[2048,512]{1,0:T(8,128)(2,1)}, u32[]{:S(2)}) copy-start(bf16[2048,512]{1,0:T(8,128)(2,1)} %param.8) | copy-start | bytes 6291460
  6.4 5.3 %copy-start.7 = (f32[4,128,128]{2,1,0:T(8,128)}, f32[4,128,128]{2,1,0:T(8,128)S(1)}, u32[]{:S(2)}) copy-start(f32[4,128,128]{2,1,0:T(8,128)S(1)} %fusion.26) | copy-start | bytes 786436
  6.4 59.6 %collective-permute-start = (f32[4,128,128]{2,1,0:T(8,128)S(1)}, f32[4,128,128]{2,1,0:T(8,128)}, u32[]{:S(2)}, u32[]{:S(2)}) collective-permute-start(f32[4,128,128]{2,1,0:T(8,128)S(1)} %fusion.26), channel_id=1, source_target_pairs={{0,1},{1,0},{2,3},{3,2},{4,5},{5,4},{6,7},{7,6},{8,9},{9,8},{10,11... | collective-permute-start | bytes 786440 | tf_op jit(solution)/shard_map/ppermute | solution.py:17
  8.6 5.2 %slice-start.3 = ((bf16[2048,512]{1,0:T(8,128)(2,1)}), bf16[1536,512]{1,0:T(8,128)(2,1)S(1)}, s32[]{:S(2)}) async-start(bf16[2048,512]{1,0:T(8,128)(2,1)} %param.8), calls=%async_computation.4 | async-start | bytes 3145728 | tf_op jit(solution)/shard_map/slice | solution.py:88
  8.7 6.7 %slice-start = ((bf16[2048,512]{1,0:T(8,128)(2,1)}), bf16[1536,512]{1,0:T(8,128)(2,1)S(1)}, s32[]{:S(2)}) async-start(bf16[2048,512]{1,0:T(8,128)(2,1)} %param.7), calls=%async_computation.1 | async-start | bytes 3145728 | tf_op jit(solution)/shard_map/slice | solution.py:87
  13.8 6.3 %copy-start.10 = (s32[32]{0:T(128)S(1)}, s32[32]{0:T(128)}, u32[]{:S(2)}) copy-start(s32[32]{0:T(128)} %param.10) | copy-start | bytes 388
  15.4 3.0 %copy-start.5 = (bf16[512,512]{1,0:T(8,128)(2,1)S(1)}, bf16[512,512]{1,0:T(8,128)(2,1)}, u32[]{:S(2)}) copy-start(bf16[512,512]{1,0:T(8,128)(2,1)} %get-tuple-element.17) | copy-start | bytes 1572868
  26.4 7.1 %copy-start.3 = (bf16[2048,512]{1,0:T(8,128)(2,1)S(1)}, bf16[2048,512]{1,0:T(8,128)(2,1)}, u32[]{:S(2)}) copy-start(bf16[2048,512]{1,0:T(8,128)(2,1)} %param.8) | copy-start | bytes 6291460
  61.7 4.3 %copy-start.8 = (f32[4,128,128]{2,1,0:T(8,128)S(1)}, f32[4,128,128]{2,1,0:T(8,128)}, u32[]{:S(2)}) copy-start(f32[4,128,128]{2,1,0:T(8,128)} %copy-done.7) | copy-start | bytes 786436
  66.1 6.7 %slice-start.1 = ((bf16[2048,512]{1,0:T(8,128)(2,1)}), bf16[1024,512]{1,0:T(8,128)(2,1)S(1)}, s32[]{:S(2)}) async-start(bf16[2048,512]{1,0:T(8,128)(2,1)} %param.7), calls=%async_computation.2 | async-start | bytes 2097152 | tf_op jit(solution)/shard_map/slice | solution.py:87
  67.2 9.3 %copy-start.6 = (f32[4,128,128]{2,1,0:T(8,128)}, f32[4,128,128]{2,1,0:T(8,128)S(1)}, u32[]{:S(2)}) copy-start(f32[4,128,128]{2,1,0:T(8,128)S(1)} %add.386) | copy-start | bytes 786436
  67.2 9.6 %collective-permute-start.1 = (f32[4,128,128]{2,1,0:T(8,128)S(1)}, f32[4,128,128]{2,1,0:T(8,128)}, u32[]{:S(2)}, u32[]{:S(2)}) collective-permute-start(f32[4,128,128]{2,1,0:T(8,128)S(1)} %add.386), channel_id=1, source_target_pairs={{0,2},{1,3},{2,0},{3,1},{4,6},{5,7},{6,4},{7,5},{8,10},{9,11},{10,... | collective-permute-start | bytes 786440 | tf_op jit(solution)/shard_map/ppermute | solution.py:17
  77.9 16.2 %collective-permute-start.2 = (f32[4,128,128]{2,1,0:T(8,128)S(1)}, f32[4,128,128]{2,1,0:T(8,128)}, u32[]{:S(2)}, u32[]{:S(2)}) collective-permute-start(f32[4,128,128]{2,1,0:T(8,128)S(1)} %add.388), channel_id=1, source_target_pairs={{0,4},{1,5},{2,6},{3,7},{4,0},{5,1},{6,2},{7,3},{8,12},{9,13},{10,... | collective-permute-start | bytes 786440 | tf_op jit(solution)/shard_map/ppermute | solution.py:17
  79.6 11.7 %slice-start.2 = ((bf16[2048,512]{1,0:T(8,128)(2,1)}), bf16[512,512]{1,0:T(8,128)(2,1)S(1)}, s32[]{:S(2)}) async-start(bf16[2048,512]{1,0:T(8,128)(2,1)} %param.7), calls=%async_computation.3 | async-start | bytes 1048576 | tf_op jit(solution)/shard_map/slice | solution.py:87
  89.2 3.1 %slice-start.4 = ((bf16[2048,512]{1,0:T(8,128)(2,1)}), bf16[512,512]{1,0:T(8,128)(2,1)S(1)}, s32[]{:S(2)}) async-start(bf16[2048,512]{1,0:T(8,128)(2,1)} %param.8), calls=%async_computation.5 | async-start | bytes 1048576 | tf_op jit(solution)/shard_map/slice | solution.py:88
  95.1 15.2 %collective-permute-start.3 = (f32[4,128,128]{2,1,0:T(8,128)S(1)}, f32[4,128,128]{2,1,0:T(8,128)S(1)}, u32[]{:S(2)}, u32[]{:S(2)}) collective-permute-start(f32[4,128,128]{2,1,0:T(8,128)S(1)} %add.390), channel_id=1, source_target_pairs={{0,8},{1,9},{2,10},{3,11},{4,12},{5,13},{6,14},{7,15},{8,0},{9,1},... | collective-permute-start | bytes 786440 | tf_op jit(solution)/shard_map/ppermute | solution.py:17
  111.1 17.2 %collective-permute-start.4 = (f32[4,128,128]{2,1,0:T(8,128)}, f32[4,128,128]{2,1,0:T(8,128)}, u32[]{:S(2)}, u32[]{:S(2)}) collective-permute-start(f32[4,128,128]{2,1,0:T(8,128)} %add.392), channel_id=1, source_target_pairs={{0,16},{1,17},{2,18},{3,19},{4,20},{5,21},{6,22},{7,23},{8,24},{9,... | collective-permute-start | bytes 786440 | tf_op jit(solution)/shard_map/ppermute | solution.py:17
  116.1 12.1 %copy-start.4 = (bf16[2048,512]{1,0:T(8,128)(2,1)S(1)}, bf16[2048,512]{1,0:T(8,128)(2,1)}, u32[]{:S(2)}) copy-start(bf16[2048,512]{1,0:T(8,128)(2,1)} %param.6) | copy-start | bytes 6291460
  135.7 11.3 %all-to-all-start = ((f32[8,1,2048]{2,1,0:T(1,128)}), f32[8,1,2048]{2,1,0:T(1,128)S(1)}, u32[]{:S(2)}, u32[]{:S(2)}) async-start(f32[8,1,2048]{2,1,0:T(1,128)} %broadcast_in_dim.172), calls=%async_computation | async-start | bytes 131072 | tf_op jit(solution)/shard_map/all_to_all | solution.py:22
  141.5 5.5 %copy-start.9 = (f32[512]{0:T(512)S(1)}, f32[512]{0:T(512)}, u32[]{:S(2)}) copy-start(f32[512]{0:T(512)} %param.11) | copy-start | bytes 6148
  147.0 5.1 %copy-start.1 = (f32[4,9]{1,0:T(4,128)S(1)}, f32[4,9]{1,0:T(4,128)}, u32[]{:S(2)}) copy-start(f32[4,9]{1,0:T(4,128)} %param.9) | copy-start | bytes 436
where the time goes:
time: 153 us; the launch traced here: 152 us
  matrix products  53 us (35%)
  local copies, waits for them, and re-layouts  32.9 us (22%)
  other arithmetic  29.6 us (19%)
  starting transfers between devices  20.4 us (13%)
  waiting for transfers between devices  16 us (10%)
    dot_general x4, matrix products, shards(): jnp.einsum('hts,shd->thd', rounded, value_span, preferred_element_type=jn...  43.8 us
    select_n x4, other arithmetic, tile_weights(): member = jnp.where(level_ids == level_num, 1.0, 0.0).astype(effective.dtype)  19.5 us
    unnamed x32, local copies, waits for them, and re-layouts  16.1 us
    ppermute x5, waiting for transfers between devices, partner(): lax.ppermute(value, axis, [(i, i ^ 1 << apart) for i in range(lax.axis_si...  16 us
    ppermute x5, starting transfers between devices, partner(): lax.ppermute(value, axis, [(i, i ^ 1 << apart) for i in range(lax.axis_si...  14.6 us
    dot_general x1, matrix products, shards(): jnp.einsum('thd,hde->the', query_rows.astype(jnp.float32), distant, preci...  6.71 us
    all_to_all x1, starting transfers between devices, copy_for_each(): lax.all_to_all(jnp.broadcast_to(value[None], (length, *value.shape)), axi...  5.84 us
    add x1, local copies, waits for them, and re-layouts, shards(): combined = (nearby + remote).reshape(seg_length, heads_here * HEAD_DIM)  5.45 us
  transfers between devices with their start and end apart: 6, of which 2 were waited for; matrix products, arithmetic and copies ran while one was open for 61% of the time, Pallas kernels for 0%

commit v1 on v0

v1 whole, which is shorter than its diff:
```python
import functools

import jax
import jax.numpy as jnp
import numpy as np
from jax import lax
from jax.experimental import pallas as pl
from jax.experimental.pallas import tpu as pltpu
from jax.sharding import PartitionSpec as P

HEAD_DIM = 128
LEAF = 256
LEAVES = 8
D = 4096
HEADS_HERE = 4
SEG = LEAF * LEAVES
WIDTH = HEADS_HERE * HEAD_DIM
NX, NZ, NH = 4, 8, 8
SLICE = HEAD_DIM // NZ
CHUNKS = 2
ROWS = SEG // CHUNKS
EPSILON = 1e-06
MESH = pl.DeviceIdType.MESH
SCALES = [float(np.float32(1.0) / np.sqrt(np.float32(LEAF * 2 ** max(l - 1, 0)))) for l in range(9)]

NT = (((1,), (1,)), ((), ()))
TN = (((0,), (0,)), ((), ()))


def dot(a, b, dims=(((1,), (0,)), ((), ()))):
    return lax.dot_general(a, b, dims, preferred_element_type=jnp.float32)


def fenwick(states, one, two, four=None):
    out = []
    pair = states[0] + states[1]
    out.append(None)
    out.append(one * states[0])
    out.append(two * pair)
    out.append(out[2] + one * states[2])
    if four is None:
        return out
    pair_b = states[4] + states[5]
    quad = four * (pair + (states[2] + states[3]))
    out.append(quad)
    out.append(quad + one * states[4])
    out.append(quad + two * pair_b)
    out.append(out[6] + one * states[6])
    return out


def kernel(
    q_hbm, k_hbm, v_hbm, table, head_table, gain, out_ref,
    q, k, v, comb, leaf_state, local, own, xrecv, total, zrecv, csend, carry, dsend, far, ssq, ssq_in,
    in_sem, x_send, x_recv, z_send, z_recv, c_send, c_recv, d_send, d_recv, s_send, s_recv,
):
    head = lax.axis_index("head")
    ctx = lax.axis_index("ctx")
    x = lax.rem(ctx, NX)
    z = lax.div(ctx, NX)

    def in_copy(i, src, dst, j):
        rows = pl.ds(pl.multiple_of(j * LEAF, LEAF), LEAF)
        return pltpu.make_async_copy(src.at[rows], dst.at[rows], in_sem.at[i, j])

    for j in range(LEAVES):
        in_copy(0, k_hbm, k, j).start()
        in_copy(1, v_hbm, v, j).start()
    for j in range(LEAVES):
        in_copy(2, q_hbm, q, j).start()

    barrier = pltpu.get_barrier_semaphore()
    for d in range(1, NX):
        pl.semaphore_signal(barrier, 1, device_id={"ctx": z * NX + lax.rem(x + d, NX)}, device_id_type=MESH)
    for d in range(1, NZ):
        pl.semaphore_signal(barrier, 1, device_id={"ctx": lax.rem(z + d, NZ) * NX + x}, device_id_type=MESH)
    for d in range(1, NH):
        pl.semaphore_signal(barrier, 1, device_id={"head": lax.rem(head + d, NH)}, device_id_type=MESH)

    def weight(h, level):
        return table[head_table[head * HEADS_HERE + h], level] * SCALES[level]

    def leaf_states(j, _):
        in_copy(0, k_hbm, k, j).wait()
        in_copy(1, v_hbm, v, j).wait()
        rows = pl.ds(pl.multiple_of(j * LEAF, LEAF), LEAF)
        for p in range(HEADS_HERE // 2):
            columns = slice(p * 256, p * 256 + 256)
            both = dot(k[rows, columns], v[rows, columns], TN)
            leaf_state[j, 2 * p] = both[:HEAD_DIM, :HEAD_DIM]
            leaf_state[j, 2 * p + 1] = both[HEAD_DIM:, HEAD_DIM:]
        return 0

    lax.fori_loop(0, LEAVES, leaf_states, 0)
    for h in range(HEADS_HERE):
        s = [leaf_state[j, h] for j in range(LEAVES)]
        own[h] = ((s[0] + s[1]) + (s[2] + s[3])) + ((s[4] + s[5]) + (s[6] + s[7]))

    pl.semaphore_wait(barrier, NX + NZ + NH - 3)

    def x_copy(d):
        to = lax.rem(x + d, NX)
        return pltpu.make_async_remote_copy(
            own.at[to], xrecv.at[x], x_send.at[d], x_recv.at[d],
            device_id={"ctx": z * NX + to}, device_id_type=MESH)

    def z_copy(d):
        to = lax.rem(z + d, NZ)
        return pltpu.make_async_remote_copy(
            total.at[pl.ds(pl.multiple_of(to * SLICE, SLICE), SLICE)], zrecv.at[z], z_send.at[d], z_recv.at[d],
            device_id={"ctx": to * NX + x}, device_id_type=MESH)

    def c_copy(d):
        to = lax.rem(z + d, NZ)
        return pltpu.make_async_remote_copy(
            csend.at[to], carry.at[pl.ds(pl.multiple_of(z * SLICE, SLICE), SLICE)], c_send.at[d], c_recv.at[d],
            device_id={"ctx": to * NX + x}, device_id_type=MESH)

    def d_copy(d):
        to = lax.rem(x + d, NX)
        return pltpu.make_async_remote_copy(
            dsend.at[to], far.at[x], d_send.at[d], d_recv.at[d],
            device_id={"ctx": z * NX + to}, device_id_type=MESH)

    for d in (2, 1, 3):
        x_copy(d).start()
    xrecv[x] = own[x]

    for h in range(HEADS_HERE):
        s = [leaf_state[j, h] for j in range(LEAVES)]
        sums = fenwick(s, weight(h, 1), weight(h, 2), weight(h, 3))
        local[0, h] = jnp.zeros((HEAD_DIM, HEAD_DIM), jnp.bfloat16)
        for j in range(1, LEAVES):
            local[j, h] = sums[j].astype(jnp.bfloat16)

    causal = lax.broadcasted_iota(jnp.int32, (LEAF, LEAF), 1) <= lax.broadcasted_iota(jnp.int32, (LEAF, LEAF), 0)

    def near(j, _):
        in_copy(2, q_hbm, q, j).wait()
        rows = pl.ds(pl.multiple_of(j * LEAF, LEAF), LEAF)
        for h in range(HEADS_HERE):
            columns = slice(h * HEAD_DIM, (h + 1) * HEAD_DIM)
            qs = q[rows, columns]
            scores = dot(qs, k[rows, columns], NT)
            rounded = jnp.where(causal, scores * weight(h, 0), 0.0).astype(jnp.bfloat16)
            comb[rows, columns] = dot(rounded, v[rows, columns]) + dot(qs, local[j, h])
        return 0

    lax.fori_loop(0, 3, near, 0)

    for d in range(1, NX):
        x_copy(d).wait_recv()
    total[...] = (xrecv[0] + xrecv[1]) + (xrecv[2] + xrecv[3])
    for d in (4, 3, 5, 2, 6, 1, 7):
        z_copy(d).start()
    zrecv[z] = total[pl.ds(pl.multiple_of(z * SLICE, SLICE), SLICE), :]

    lax.fori_loop(3, 5, near, 0)

    for d in range(1, NZ):
        z_copy(d).wait_recv()
    sums = fenwick([zrecv[i] for i in range(NZ)], weight(x, 6), weight(x, 7), weight(x, 8))
    csend[0] = jnp.zeros((SLICE, HEAD_DIM), jnp.float32)
    for i in range(1, NZ):
        csend[i] = sums[i]
    for d in (4, 3, 5, 2, 6, 1, 7):
        c_copy(d).start()
    carry[pl.ds(pl.multiple_of(z * SLICE, SLICE), SLICE), :] = csend[z]

    lax.fori_loop(5, 7, near, 0)

    for d in range(1, NZ):
        c_copy(d).wait_recv()
    sums = fenwick([xrecv[i] for i in range(NX)], weight(x, 4), weight(x, 5))
    dsend[0] = carry[...]
    for i in range(1, NX):
        dsend[i] = carry[...] + sums[i]
    for d in (2, 1, 3):
        d_copy(d).start()
    far[x] = dsend[x]

    lax.fori_loop(7, LEAVES, near, 0)

    for d in range(1, NX):
        d_copy(d).wait_recv()

    zero = jnp.zeros((HEAD_DIM, HEAD_DIM), jnp.float32)
    high, low = [], []
    for p in range(HEADS_HERE // 2):
        block = jnp.concatenate([
            jnp.concatenate([far[2 * p], zero], axis=1),
            jnp.concatenate([zero, far[2 * p + 1]], axis=1)], axis=0)
        top = block.astype(jnp.bfloat16)
        high.append(top)
        low.append((block - top.astype(jnp.float32)).astype(jnp.bfloat16))
    ones = jnp.ones((8, HEAD_DIM), jnp.bfloat16)

    def s_copy(c, d):
        return pltpu.make_async_remote_copy(
            ssq.at[c], ssq_in.at[c, d], s_send.at[c, d], s_recv.at[c, d],
            device_id={"head": lax.rem(head + d, NH)}, device_id_type=MESH)

    for c in range(CHUNKS):
        for j in range(ROWS // LEAF):
            rows = slice(c * ROWS + j * LEAF, c * ROWS + (j + 1) * LEAF)
            squares = None
            for p in range(HEADS_HERE // 2):
                columns = slice(p * 256, p * 256 + 256)
                qs = q[rows, columns]
                value = comb[rows, columns] + (dot(qs, high[p]) + dot(qs, low[p]))
                comb[rows, columns] = value
                square = value * value
                square = square[:, :HEAD_DIM] + square[:, HEAD_DIM:]
                squares = square if squares is None else squares + square
            top = squares.astype(jnp.bfloat16)
            rest = (squares - top.astype(jnp.float32)).astype(jnp.bfloat16)
            line = dot(ones, top, NT) + dot(ones, rest, NT)
            ssq[c, 2 * j:2 * j + 1] = line[:1, :HEAD_DIM]
            ssq[c, 2 * j + 1:2 * j + 2] = line[:1, HEAD_DIM:]
        for d in range(1, NH):
            s_copy(c, d).start()

    for c in range(CHUNKS):
        for d in range(1, NH):
            s_copy(c, d).wait_recv()
        a = [ssq[c]] + [ssq_in[c, d] for d in range(1, NH)]
        whole = ((a[0] + a[1]) + (a[2] + a[3])) + ((a[4] + a[5]) + (a[6] + a[7]))
        inverse = lax.rsqrt(whole * (1.0 / D) + EPSILON).T
        for i in range(ROWS // HEAD_DIM):
            rows = slice(c * ROWS + i * HEAD_DIM, c * ROWS + (i + 1) * HEAD_DIM)
            out_ref[rows] = (comb[rows] * inverse[:, i:i + 1] * gain[...]).astype(jnp.bfloat16)

    for d in range(1, NX):
        x_copy(d).wait_send()
        d_copy(d).wait_send()
    for d in range(1, NZ):
        z_copy(d).wait_send()
        c_copy(d).wait_send()
    for c in range(CHUNKS):
        for d in range(1, NH):
            s_copy(c, d).wait_send()


def shards(queries, keys, values, level_table, head_table, gain):
    f32, bf16 = jnp.float32, jnp.bfloat16
    dma = pltpu.SemaphoreType.DMA
    square = (HEAD_DIM, HEAD_DIM)
    anywhere = pl.BlockSpec(memory_space=pltpu.HBM)
    smem = pl.BlockSpec(memory_space=pltpu.SMEM)
    vmem = pl.BlockSpec(memory_space=pltpu.VMEM)
    return pl.pallas_call(
        kernel,
        out_shape=jax.ShapeDtypeStruct((SEG, WIDTH), bf16),
        in_specs=[anywhere, anywhere, anywhere, smem, smem, vmem],
        out_specs=vmem,
        scratch_shapes=[
            pltpu.VMEM((SEG, WIDTH), bf16),
            pltpu.VMEM((SEG, WIDTH), bf16),
            pltpu.VMEM((SEG, WIDTH), bf16),
            pltpu.VMEM((SEG, WIDTH), f32),
            pltpu.VMEM((LEAVES, HEADS_HERE, *square), f32),
            pltpu.VMEM((LEAVES, HEADS_HERE, *square), bf16),
            pltpu.VMEM((HEADS_HERE, *square), f32),
            pltpu.VMEM((NX, *square), f32),
            pltpu.VMEM(square, f32),
            pltpu.VMEM((NZ, SLICE, HEAD_DIM), f32),
            pltpu.VMEM((NZ, SLICE, HEAD_DIM), f32),
            pltpu.VMEM(square, f32),
            pltpu.VMEM((NX, *square), f32),
            pltpu.VMEM((HEADS_HERE, *square), f32),
            pltpu.VMEM((CHUNKS, 8, HEAD_DIM), f32),
            pltpu.VMEM((CHUNKS, NH, 8, HEAD_DIM), f32),
            dma((3, LEAVES)),
            dma((NX,)), dma((NX,)),
            dma((NZ,)), dma((NZ,)),
            dma((NZ,)), dma((NZ,)),
            dma((NX,)), dma((NX,)),
            dma((CHUNKS, NH)), dma((CHUNKS, NH)),
        ],
        compiler_params=pltpu.CompilerParams(
            collective_id=0, has_side_effects=True, vmem_limit_bytes=40 * 1024 * 1024),
        name="attend",
    )(queries, keys, values, level_table, head_table, gain.reshape(1, WIDTH))


def solution(mesh):
    return jax.shard_map(
        shards,
        mesh=mesh,
        in_specs=(P("ctx", "head"), P("ctx", "head"), P("ctx", "head"), P(), P(), P("head")),
        out_specs=P("ctx", "head"),
        check_vma=False,
    )
```

time: 153 us -> 45.8 us (0.30)
  matrix products: 53 us -> 0 us
  Pallas kernels: 0 us -> 37.5 us
  other arithmetic: 29.6 us -> 0 us
  local copies, waits for them, and re-layouts: 32.9 us -> 8.11 us
  starting transfers between devices: 20.4 us -> 0 us
  waiting for transfers between devices: 16 us -> 0 us
    dot_general x7 -> x0, matrix products: 53 us -> none  [the longest x4 43.8 us: shards(): jnp.einsum('hts,shd->thd', rounded, value_span, preferred_element_type=jn...]
    pallas_call x0 -> x1, Pallas kernels: none -> 37.5 us  [shards(): pl.pallas_call(kernel, out_shape=jax.ShapeDtypeStruct((SEG, WIDTH), bf16)...]
    select_n x11 -> x0, other arithmetic: 19.5 us -> none  [the longest x4 19.5 us: tile_weights(): member = jnp.where(level_ids == level_num, 1.0, 0.0).astype(effective.dtype)]
    ppermute x5 -> x0, waiting for transfers between devices: 16 us -> none  [partner(): lax.ppermute(value, axis, [(i, i ^ 1 << apart) for i in range(lax.axis_si...]
    ppermute x5 -> x0, starting transfers between devices: 14.6 us -> none  [partner(): lax.ppermute(value, axis, [(i, i ^ 1 << apart) for i in range(lax.axis_si...]
    unnamed x32 -> x13, local copies, waits for them, and re-layouts: 16.1 us -> 8.11 us
    all_to_all x1 -> x0, starting transfers between devices: 5.84 us -> none  [copy_for_each(): lax.all_to_all(jnp.broadcast_to(value[None], (length, *value.shape)), axi...]
    add x1 -> x0, local copies, waits for them, and re-layouts: 5.45 us -> none  [shards(): combined = (nearby + remote).reshape(seg_length, heads_here * HEAD_DIM)]
  transfers between devices with their start and end apart: 6 -> 0, of which waited for: 2 -> 0; matrix products, arithmetic and copies ran while one was open for 61% -> 0% of each run, Pallas kernels for 0% -> 0%
where the time goes in v1:
time: 45.8 us; the launch traced here: 45.6 us
  Pallas kernels  37.5 us (82%)
  local copies, waits for them, and re-layouts  8.11 us (18%)
    pallas_call x1, Pallas kernels, shards(): pl.pallas_call(kernel, out_shape=jax.ShapeDtypeStruct((SEG, WIDTH), bf16)...  37.5 us
    unnamed x13, local copies, waits for them, and re-layouts  8.11 us

profile of v1, /device:TPU:1, one launch (start us, length us, event | category | flops | bytes accessed | tf_op | source)
XLA Modules:
  0.0 45.6 jit_solution(14951436934032807647)
XLA Ops:
  0.0 0.0 copy-start
  0.0 1.6 %copy-done = bf16[2048,512]{1,0:T(8,128)(2,1)S(1)} copy-done((bf16[2048,512]{1,0:T(8,128)(2,1)S(1)}, bf16[2048,512]{1,0:T(8,128)(2,1)}, u32[]{:S(2)}) %copy-start) | copy-done | bytes 2097176
  1.6 0.0 copy-start.1
  1.6 1.6 %copy-done.1 = bf16[2048,512]{1,0:T(8,128)(2,1)S(1)} copy-done((bf16[2048,512]{1,0:T(8,128)(2,1)S(1)}, bf16[2048,512]{1,0:T(8,128)(2,1)}, u32[]{:S(2)}) %copy-start.1) | copy-done | bytes 2097176
  3.2 0.0 copy-start.2
  3.2 1.6 %copy-done.2 = bf16[2048,512]{1,0:T(8,128)(2,1)S(1)} copy-done((bf16[2048,512]{1,0:T(8,128)(2,1)S(1)}, bf16[2048,512]{1,0:T(8,128)(2,1)}, u32[]{:S(2)}) %copy-start.2) | copy-done | bytes 2097176
  4.8 0.0 copy-start.3
  4.8 0.7 %copy-done.3 = f32[4,9]{1,0:T(4,128)S(1)} copy-done((f32[4,9]{1,0:T(4,128)S(1)}, f32[4,9]{1,0:T(4,128)}, u32[]{:S(2)}) %copy-start.3) | copy-done | bytes 168
  5.5 0.0 copy-start.4
  5.5 0.7 %copy-done.4 = f32[512]{0:T(512)S(1)} copy-done((f32[512]{0:T(512)S(1)}, f32[512]{0:T(512)}, u32[]{:S(2)}) %copy-start.4) | copy-done | bytes 2072
  6.1 0.0 copy-start.5
  6.1 0.7 %copy-done.5 = s32[32]{0:T(128)S(1)} copy-done((s32[32]{0:T(128)S(1)}, s32[32]{0:T(128)}, u32[]{:S(2)}) %copy-start.5) | copy-done | bytes 152
  6.8 37.5 %attend.1 = bf16[2048,512]{1,0:T(8,128)(2,1)S(1)} custom-call(bf16[2048,512]{1,0:T(8,128)(2,1)S(1)} %copy-done, bf16[2048,512]{1,0:T(8,128)(2,1)S(1)} %copy-done.1, bf16[2048,512]{1,0:T(8,128)(2,1)S(1)} %copy-done.2, f32[4,9]{1,0:T(4,128)S(1)} %copy-done.3, s32[32]{0:T(128)S(1)} %copy-done.5, f32[1,512]{1,0:T(1,128)S(1)} %bitcast.1), custom_call_target="tpu_custom_call" | custom-call | tf_op jit(solution)/shard_map/attend/pallas_call | solution.py:251
  44.3 1.3 %copy.8 = bf16[2048,512]{1,0:T(8,128)(2,1)} copy(bf16[2048,512]{1,0:T(8,128)(2,1)S(1)} %attend.1) | data formatting | bytes 4194304
Async XLA Ops:
  0.0 1.6 %copy-start = (bf16[2048,512]{1,0:T(8,128)(2,1)S(1)}, bf16[2048,512]{1,0:T(8,128)(2,1)}, u32[]{:S(2)}) copy-start(bf16[2048,512]{1,0:T(8,128)(2,1)} %q_hbm.1) | copy-start | bytes 6291460
  1.6 1.6 %copy-start.1 = (bf16[2048,512]{1,0:T(8,128)(2,1)S(1)}, bf16[2048,512]{1,0:T(8,128)(2,1)}, u32[]{:S(2)}) copy-start(bf16[2048,512]{1,0:T(8,128)(2,1)} %k_hbm.1) | copy-start | bytes 6291460
  3.2 1.6 %copy-start.2 = (bf16[2048,512]{1,0:T(8,128)(2,1)S(1)}, bf16[2048,512]{1,0:T(8,128)(2,1)}, u32[]{:S(2)}) copy-start(bf16[2048,512]{1,0:T(8,128)(2,1)} %v_hbm.1) | copy-start | bytes 6291460
  4.8 0.7 %copy-start.3 = (f32[4,9]{1,0:T(4,128)S(1)}, f32[4,9]{1,0:T(4,128)}, u32[]{:S(2)}) copy-start(f32[4,9]{1,0:T(4,128)} %table.1) | copy-start | bytes 436
  5.5 0.7 %copy-start.4 = (f32[512]{0:T(512)S(1)}, f32[512]{0:T(512)}, u32[]{:S(2)}) copy-start(f32[512]{0:T(512)} %param.11) | copy-start | bytes 6148
  6.1 0.7 %copy-start.5 = (s32[32]{0:T(128)S(1)}, s32[32]{0:T(128)}, u32[]{:S(2)}) copy-start(s32[32]{0:T(128)} %head_table.1) | copy-start | bytes 388

commit v2 on v1

--- a/solution.py
+++ b/solution.py
@@ -15,8 +15,9 @@
 HEADS_HERE = 4
 SEG = LEAF * LEAVES
 WIDTH = HEADS_HERE * HEAD_DIM
-NX, NZ, NH = 4, 8, 8
-SLICE = HEAD_DIM // NZ
+NX, GROUPS, NH = 4, 4, 8
+HALF = HEAD_DIM // 2
+AROUND = [(1, 2), (1, 1), (1, 3), (0, 2), (1, 0), (0, 1), (0, 3)]
 CHUNKS = 2
 ROWS = SEG // CHUNKS
 EPSILON = 1e-06
@@ -51,13 +52,16 @@
 
 def kernel(
     q_hbm, k_hbm, v_hbm, table, head_table, gain, out_ref,
-    q, k, v, comb, leaf_state, local, own, xrecv, total, zrecv, csend, carry, dsend, far, ssq, ssq_in,
-    in_sem, x_send, x_recv, z_send, z_recv, c_send, c_recv, d_send, d_recv, s_send, s_recv,
+    q, k, v, comb, leaf_state, local, own, xrecv, total, earlier, dsend, far, ssq, ssq_in,
+    in_sem, x_send, x_recv, t_send, t_recv, d_send, d_recv, s_send, s_recv, ready,
 ):
     head = lax.axis_index("head")
     ctx = lax.axis_index("ctx")
     x = lax.rem(ctx, NX)
     z = lax.div(ctx, NX)
+    group = lax.div(z, 2)
+    odd = lax.rem(z, 2)
+    part = lax.rem(odd + lax.div(z, 4), 2)
 
     def in_copy(i, src, dst, j):
         rows = pl.ds(pl.multiple_of(j * LEAF, LEAF), LEAF)
@@ -66,14 +70,23 @@
     for j in range(LEAVES):
         in_copy(0, k_hbm, k, j).start()
         in_copy(1, v_hbm, v, j).start()
-    for j in range(LEAVES):
-        in_copy(2, q_hbm, q, j).start()
-
+
+    def near_by(dz, dx):
+        to_odd, to_x = lax.rem(odd + dz, 2), lax.rem(x + dx, NX)
+        return to_odd, to_x, {"ctx": (2 * group + to_odd) * NX + to_x}
+
+    def counterpart(g):
+        return {"ctx": (2 * g + lax.rem(part + g // 2, 2)) * NX + x}
+
+    for g in range(GROUPS - 1):
+        earlier[g] = jnp.zeros((HALF, HEAD_DIM), jnp.float32)
     barrier = pltpu.get_barrier_semaphore()
-    for d in range(1, NX):
-        pl.semaphore_signal(barrier, 1, device_id={"ctx": z * NX + lax.rem(x + d, NX)}, device_id_type=MESH)
-    for d in range(1, NZ):
-        pl.semaphore_signal(barrier, 1, device_id={"ctx": lax.rem(z + d, NZ) * NX + x}, device_id_type=MESH)
+    for dz, dx in AROUND:
+        pl.semaphore_signal(barrier, 1, device_id=near_by(dz, dx)[2], device_id_type=MESH)
+    for g in range(1, GROUPS):
+        @pl.when(group < g)
+        def _():
+            pl.semaphore_signal(barrier, 1, device_id=counterpart(g), device_id_type=MESH)
     for d in range(1, NH):
         pl.semaphore_signal(barrier, 1, device_id={"head": lax.rem(head + d, NH)}, device_id_type=MESH)
 
@@ -94,37 +107,43 @@
     lax.fori_loop(0, LEAVES, leaf_states, 0)
     for h in range(HEADS_HERE):
         s = [leaf_state[j, h] for j in range(LEAVES)]
-        own[h] = ((s[0] + s[1]) + (s[2] + s[3])) + ((s[4] + s[5]) + (s[6] + s[7]))
-
-    pl.semaphore_wait(barrier, NX + NZ + NH - 3)
-
-    def x_copy(d):
-        to = lax.rem(x + d, NX)
-        return pltpu.make_async_remote_copy(
-            own.at[to], xrecv.at[x], x_send.at[d], x_recv.at[d],
-            device_id={"ctx": z * NX + to}, device_id_type=MESH)
-
-    def z_copy(d):
-        to = lax.rem(z + d, NZ)
-        return pltpu.make_async_remote_copy(
-            total.at[pl.ds(pl.multiple_of(to * SLICE, SLICE), SLICE)], zrecv.at[z], z_send.at[d], z_recv.at[d],
-            device_id={"ctx": to * NX + x}, device_id_type=MESH)
-
-    def c_copy(d):
-        to = lax.rem(z + d, NZ)
-        return pltpu.make_async_remote_copy(
-            csend.at[to], carry.at[pl.ds(pl.multiple_of(z * SLICE, SLICE), SLICE)], c_send.at[d], c_recv.at[d],
-            device_id={"ctx": to * NX + x}, device_id_type=MESH)
-
-    def d_copy(d):
-        to = lax.rem(x + d, NX)
-        return pltpu.make_async_remote_copy(
-            dsend.at[to], far.at[x], d_send.at[d], d_recv.at[d],
-            device_id={"ctx": z * NX + to}, device_id_type=MESH)
-
-    for d in (2, 1, 3):
-        x_copy(d).start()
-    xrecv[x] = own[x]
+        whole = ((s[0] + s[1]) + (s[2] + s[3])) + ((s[4] + s[5]) + (s[6] + s[7]))
+        own[h, 0] = whole[:HALF]
+        own[h, 1] = whole[HALF:]
+
+    pl.semaphore_wait(barrier, len(AROUND) + NH - 1 + group)
+    for g in range(GROUPS - 1):
+        @pl.when(group > g)
+        def _():
+            pl.semaphore_signal(ready.at[group], 1, device_id=counterpart(g), device_id_type=MESH)
+
+    def x_copy(dz, dx):
+        to_odd, to_x, to = near_by(dz, dx)
+        return pltpu.make_async_remote_copy(
+            own.at[to_x, lax.rem(to_odd + lax.div(z, 4), 2)], xrecv.at[odd, x],
+            x_send.at[dz, dx], x_recv.at[dz, dx], device_id=to, device_id_type=MESH)
+
+    def t_copy(g):
+        return pltpu.make_async_remote_copy(
+            total, earlier.at[group], t_send.at[g], t_recv.at[group],
+            device_id=counterpart(g), device_id_type=MESH)
+
+    def t_arrival(g):
+        return pltpu.make_async_remote_copy(
+            total, earlier.at[g], t_send.at[g], t_recv.at[g],
+            device_id=counterpart(g), device_id_type=MESH)
+
+    def d_copy(dz, dx):
+        to_odd, to_x, to = near_by(dz, dx)
+        return pltpu.make_async_remote_copy(
+            dsend.at[to_odd, to_x], far.at[x, part],
+            d_send.at[dz, dx], d_recv.at[dz, dx], device_id=to, device_id_type=MESH)
+
+    for dz, dx in AROUND:
+        x_copy(dz, dx).start()
+    xrecv[odd, x] = own[x, part]
+    for j in range(LEAVES):
+        in_copy(2, q_hbm, q, j).start()
 
     for h in range(HEADS_HERE):
         s = [leaf_state[j, h] for j in range(LEAVES)]
@@ -148,48 +167,51 @@
 
     lax.fori_loop(0, 3, near, 0)
 
-    for d in range(1, NX):
-        x_copy(d).wait_recv()
-    total[...] = (xrecv[0] + xrecv[1]) + (xrecv[2] + xrecv[3])
-    for d in (4, 3, 5, 2, 6, 1, 7):
-        z_copy(d).start()
-    zrecv[z] = total[pl.ds(pl.multiple_of(z * SLICE, SLICE), SLICE), :]
+    for dz, dx in AROUND:
+        x_copy(dz, dx).wait_recv()
+    row = [[xrecv[i, j] for j in range(NX)] for i in range(2)]
+    row_sum = [(r[0] + r[1]) + (r[2] + r[3]) for r in row]
+    total[...] = row_sum[0] + row_sum[1]
+    for g in range(GROUPS - 1, 0, -1):
+        @pl.when(group < g)
+        def _():
+            pl.semaphore_wait(ready.at[g], 1)
+            t_copy(g).start()
 
     lax.fori_loop(3, 5, near, 0)
 
-    for d in range(1, NZ):
-        z_copy(d).wait_recv()
-    sums = fenwick([zrecv[i] for i in range(NZ)], weight(x, 6), weight(x, 7), weight(x, 8))
-    csend[0] = jnp.zeros((SLICE, HEAD_DIM), jnp.float32)
-    for i in range(1, NZ):
-        csend[i] = sums[i]
-    for d in (4, 3, 5, 2, 6, 1, 7):
-        c_copy(d).start()
-    carry[pl.ds(pl.multiple_of(z * SLICE, SLICE), SLICE), :] = csend[z]
-
-    lax.fori_loop(5, 7, near, 0)
-
-    for d in range(1, NZ):
-        c_copy(d).wait_recv()
-    sums = fenwick([xrecv[i] for i in range(NX)], weight(x, 4), weight(x, 5))
-    dsend[0] = carry[...]
-    for i in range(1, NX):
-        dsend[i] = carry[...] + sums[i]
-    for d in (2, 1, 3):
-        d_copy(d).start()
-    far[x] = dsend[x]
-
-    lax.fori_loop(7, LEAVES, near, 0)
-
-    for d in range(1, NX):
-        d_copy(d).wait_recv()
+    for g in range(GROUPS - 1):
+        @pl.when(group > g)
+        def _():
+            t_arrival(g).wait_recv()
+    far_weight = jnp.where(group >= 2, weight(x, 8), 0.0)
+    base = (
+        (far_weight + jnp.where(group == 1, weight(x, 7), 0.0)) * earlier[0]
+        + far_weight * earlier[1]
+        + jnp.where(group == 3, weight(x, 7), 0.0) * earlier[2])
+    for i in range(2):
+        sums = fenwick(row[i], weight(x, 4), weight(x, 5))
+        if i:
+            base = base + weight(x, 6) * row_sum[0]
+        dsend[i, 0] = base
+        for j in range(1, NX):
+            dsend[i, j] = base + sums[j]
+    for dz, dx in AROUND:
+        d_copy(dz, dx).start()
+    far[x, part] = dsend[odd, x]
+
+    lax.fori_loop(5, LEAVES, near, 0)
+
+    for dz, dx in AROUND:
+        d_copy(dz, dx).wait_recv()
 
     zero = jnp.zeros((HEAD_DIM, HEAD_DIM), jnp.float32)
     high, low = [], []
+    state = [jnp.concatenate([far[h, 0], far[h, 1]], axis=0) for h in range(HEADS_HERE)]
     for p in range(HEADS_HERE // 2):
         block = jnp.concatenate([
-            jnp.concatenate([far[2 * p], zero], axis=1),
-            jnp.concatenate([zero, far[2 * p + 1]], axis=1)], axis=0)
+            jnp.concatenate([state[2 * p], zero], axis=1),
+            jnp.concatenate([zero, state[2 * p + 1]], axis=1)], axis=0)
         top = block.astype(jnp.bfloat16)
         high.append(top)
         low.append((block - top.astype(jnp.float32)).astype(jnp.bfloat16))
@@ -230,12 +252,13 @@
             rows = slice(c * ROWS + i * HEAD_DIM, c * ROWS + (i + 1) * HEAD_DIM)
             out_ref[rows] = (comb[rows] * inverse[:, i:i + 1] * gain[...]).astype(jnp.bfloat16)
 
-    for d in range(1, NX):
-        x_copy(d).wait_send()
-        d_copy(d).wait_send()
-    for d in range(1, NZ):
-        z_copy(d).wait_send()
-        c_copy(d).wait_send()
+    for dz, dx in AROUND:
+        x_copy(dz, dx).wait_send()
+        d_copy(dz, dx).wait_send()
+    for g in range(1, GROUPS):
+        @pl.when(group < g)
+        def _():
+            t_copy(g).wait_send()
     for c in range(CHUNKS):
         for d in range(1, NH):
             s_copy(c, d).wait_send()
@@ -244,13 +267,13 @@
 def shards(queries, keys, values, level_table, head_table, gain):
     f32, bf16 = jnp.float32, jnp.bfloat16
     dma = pltpu.SemaphoreType.DMA
-    square = (HEAD_DIM, HEAD_DIM)
+    square, half = (HEAD_DIM, HEAD_DIM), (HALF, HEAD_DIM)
     anywhere = pl.BlockSpec(memory_space=pltpu.HBM)
     smem = pl.BlockSpec(memory_space=pltpu.SMEM)
     vmem = pl.BlockSpec(memory_space=pltpu.VMEM)
     return pl.pallas_call(
         kernel,
-        out_shape=jax.ShapeDtypeStruct((SEG, WIDTH), bf16),
+        out_shape=pltpu.VMEM((SEG, WIDTH), bf16),
         in_specs=[anywhere, anywhere, anywhere, smem, smem, vmem],
         out_specs=vmem,
         scratch_shapes=[
@@ -260,27 +283,26 @@
             pltpu.VMEM((SEG, WIDTH), f32),
             pltpu.VMEM((LEAVES, HEADS_HERE, *square), f32),
             pltpu.VMEM((LEAVES, HEADS_HERE, *square), bf16),
-            pltpu.VMEM((HEADS_HERE, *square), f32),
-            pltpu.VMEM((NX, *square), f32),
-            pltpu.VMEM(square, f32),
-            pltpu.VMEM((NZ, SLICE, HEAD_DIM), f32),
-            pltpu.VMEM((NZ, SLICE, HEAD_DIM), f32),
-            pltpu.VMEM(square, f32),
-            pltpu.VMEM((NX, *square), f32),
-            pltpu.VMEM((HEADS_HERE, *square), f32),
+            pltpu.VMEM((HEADS_HERE, 2, *half), f32),
+            pltpu.VMEM((2, NX, *half), f32),
+            pltpu.VMEM(half, f32),
+            pltpu.VMEM((GROUPS - 1, *half), f32),
+            pltpu.VMEM((2, NX, *half), f32),
+            pltpu.VMEM((HEADS_HERE, 2, *half), f32),
             pltpu.VMEM((CHUNKS, 8, HEAD_DIM), f32),
             pltpu.VMEM((CHUNKS, NH, 8, HEAD_DIM), f32),
             dma((3, LEAVES)),
-            dma((NX,)), dma((NX,)),
-            dma((NZ,)), dma((NZ,)),
-            dma((NZ,)), dma((NZ,)),
-            dma((NX,)), dma((NX,)),
+            dma((2, NX)), dma((2, NX)),
+            dma((GROUPS,)), dma((GROUPS,)),
+            dma((2, NX)), dma((2, NX)),
             dma((CHUNKS, NH)), dma((CHUNKS, NH)),
+            pltpu.SemaphoreType.REGULAR((GROUPS,)),
         ],
         compiler_params=pltpu.CompilerParams(
             collective_id=0, has_side_effects=True, vmem_limit_bytes=40 * 1024 * 1024),
         name="attend",
-    )(queries, keys, values, level_table, head_table, gain.reshape(1, WIDTH))
+    )(*[pltpu.with_memory_space_constraint(a, pltpu.HBM) for a in
+       (queries, keys, values, level_table, head_table, gain.reshape(1, WIDTH))])
 
 
 def solution(mesh):

time: 45.8 us -> 29.9 us (0.65)
  Pallas kernels: 37.5 us -> 28.5 us
  local copies, waits for them, and re-layouts: 8.11 us -> 1.32 us
    pallas_call x1, Pallas kernels: 37.5 us -> 28.5 us  [shards(): pl.pallas_call(kernel, out_shape=pltpu.VMEM((SEG, WIDTH), bf16), in_specs...]
    unnamed x13 -> x1, local copies, waits for them, and re-layouts: 8.11 us -> 1.32 us
where the time goes in v2:
time: 29.9 us; the launch traced here: 29.8 us
  Pallas kernels  28.5 us (95%)
  local copies, waits for them, and re-layouts  1.32 us (4%)
    pallas_call x1, Pallas kernels, shards(): pl.pallas_call(kernel, out_shape=pltpu.VMEM((SEG, WIDTH), bf16), in_specs...  28.5 us
    unnamed x1, local copies, waits for them, and re-layouts  1.32 us

profile of v2, /device:TPU:1, one launch (start us, length us, event | category | flops | bytes accessed | tf_op | source)
XLA Modules:
  0.0 29.8 jit_solution(13520351576902259952)
XLA Ops:
  0.0 28.5 %attend.1 = bf16[2048,512]{1,0:T(8,128)(2,1)S(1)} custom-call(bf16[2048,512]{1,0:T(8,128)(2,1)} %q_hbm.1, bf16[2048,512]{1,0:T(8,128)(2,1)} %k_hbm.1, bf16[2048,512]{1,0:T(8,128)(2,1)} %v_hbm.1, f32[4,9]{1,0:T(4,128)} %table.1, s32[32]{0:T(128)} %head_table.1, f32[1,512]{1,0:T(1,128)} %bitcast.1), custom_call_target="tpu_custom_call" | custom-call | tf_op jit(solution)/shard_map/attend/pallas_call | solution.py:274
  28.5 1.3 %copy.8 = bf16[2048,512]{1,0:T(8,128)(2,1)} copy(bf16[2048,512]{1,0:T(8,128)(2,1)S(1)} %attend.1) | data formatting | bytes 4194304

commit v3 on v2

v3 whole, which is shorter than its diff:
```python
import functools

import jax
import jax.numpy as jnp
import numpy as np
from jax import lax
from jax.experimental import pallas as pl
from jax.experimental.pallas import tpu as pltpu
from jax.sharding import PartitionSpec as P

HEAD_DIM = 128
LEAF = 256
LEAVES = 8
D = 4096
HEADS_HERE = 4
SEG = LEAF * LEAVES
WIDTH = HEADS_HERE * HEAD_DIM
NX, GROUPS, NH = 4, 4, 8
HALF = HEAD_DIM // 2
PAIR = 2 * HEAD_DIM
CHUNK = 2 * LEAF
AROUND = [(1, 2), (1, 1), (1, 3), (0, 2), (1, 0), (0, 1), (0, 3)]
CHUNKS = 2
ROWS = SEG // CHUNKS
EPSILON = 1e-06
MESH = pl.DeviceIdType.MESH
SCALES = [float(np.float32(1.0) / np.sqrt(np.float32(LEAF * 2 ** max(l - 1, 0)))) for l in range(9)]

NT = (((1,), (1,)), ((), ()))
TN = (((0,), (0,)), ((), ()))


def dot(a, b, dims=(((1,), (0,)), ((), ()))):
    return lax.dot_general(a, b, dims, preferred_element_type=jnp.float32)


def fenwick(states, one, two, four=None):
    out = []
    pair = states[0] + states[1]
    out.append(None)
    out.append(one * states[0])
    out.append(two * pair)
    out.append(out[2] + one * states[2])
    if four is None:
        return out
    pair_b = states[4] + states[5]
    quad = four * (pair + (states[2] + states[3]))
    out.append(quad)
    out.append(quad + one * states[4])
    out.append(quad + two * pair_b)
    out.append(out[6] + one * states[6])
    return out


def kernel(
    q_hbm, k_hbm, v_hbm, table_hbm, head_table_hbm, gain_hbm, out_ref,
    table, head_table, gain, q, kv, comb, square_sum, leaf_state, local, own, xrecv, total, earlier, dsend, far,
    ssq, ssq_in, small_sem, kv_sem, q_sem, x_send, x_recv, t_send, t_recv, d_send, d_recv, s_send, s_recv, ready,
):
    head = lax.axis_index("head")
    ctx = lax.axis_index("ctx")
    x = lax.rem(ctx, NX)
    z = lax.div(ctx, NX)
    group = lax.div(z, 2)
    odd = lax.rem(z, 2)
    part = lax.rem(odd + lax.div(z, 4), 2)

    def kv_part(p, c):
        return pl.ds(c * CHUNK, CHUNK), pl.ds(p * PAIR, PAIR)

    for p in range(HEADS_HERE // 2):
        for c in range(SEG // CHUNK):
            here = kv_part(p, c)
            pltpu.make_async_copy(k_hbm.at[here], kv.at[(0, *here)], kv_sem.at[p, c]).start()
            pltpu.make_async_copy(v_hbm.at[here], kv.at[(1, *here)], kv_sem.at[p, c]).start()
    small = [
        pltpu.make_async_copy(a, b, small_sem.at[i])
        for i, (a, b) in enumerate(((table_hbm, table), (head_table_hbm, head_table), (gain_hbm, gain)))]
    for copy in small:
        copy.start()
    q_copy = pltpu.make_async_copy(q_hbm, q, q_sem)

    def near_by(dz, dx):
        to_odd, to_x = lax.rem(odd + dz, 2), lax.rem(x + dx, NX)
        return to_odd, to_x, {"ctx": (2 * group + to_odd) * NX + to_x}

    def counterpart(g):
        return {"ctx": (2 * g + lax.rem(part + g // 2, 2)) * NX + x}

    for g in range(GROUPS - 1):
        earlier[g] = jnp.zeros((HALF, HEAD_DIM), jnp.float32)
    barrier = pltpu.get_barrier_semaphore()
    for dz, dx in AROUND:
        pl.semaphore_signal(barrier, 1, device_id=near_by(dz, dx)[2], device_id_type=MESH)
    for g in range(1, GROUPS):
        @pl.when(group < g)
        def _():
            pl.semaphore_signal(barrier, 1, device_id=counterpart(g), device_id_type=MESH)
    for d in range(1, NH):
        pl.semaphore_signal(barrier, 1, device_id={"head": lax.rem(head + d, NH)}, device_id_type=MESH)

    def weight(h, level):
        return table[head_table[head * HEADS_HERE + h], level] * SCALES[level]

    def x_copy(dz, dx):
        to_odd, to_x, to = near_by(dz, dx)
        return pltpu.make_async_remote_copy(
            own.at[to_x, lax.rem(to_odd + lax.div(z, 4), 2)], xrecv.at[odd, x],
            x_send, x_recv, device_id=to, device_id_type=MESH)

    def t_copy(g):
        return pltpu.make_async_remote_copy(
            total, earlier.at[group], t_send.at[g - 1], t_recv.at[group],
            device_id=counterpart(g), device_id_type=MESH)

    def d_copy(dz, dx):
        to_odd, to_x, to = near_by(dz, dx)
        return pltpu.make_async_remote_copy(
            dsend.at[to_odd, to_x], far.at[x, part],
            d_send, d_recv.at[dx], device_id=to, device_id_type=MESH)

    def pair_states(p):
        columns = slice(p * PAIR, (p + 1) * PAIR)
        whole = None
        for c in range(SEG // CHUNK):
            arrived = kv.at[(slice(None), *kv_part(p, c))]
            pltpu.make_async_copy(arrived, arrived, kv_sem.at[p, c]).wait()
            for j in range(c * CHUNK // LEAF, (c + 1) * CHUNK // LEAF):
                rows = slice(j * LEAF, (j + 1) * LEAF)
                both = dot(kv[0, rows, columns], kv[1, rows, columns], TN)
                two = both[:HEAD_DIM, :HEAD_DIM], both[HEAD_DIM:, HEAD_DIM:]
                for i in range(2):
                    leaf_state[j, 2 * p + i] = two[i]
                whole = two if whole is None else [m + n for m, n in zip(whole, two)]
        for i in range(2):
            own[2 * p + i, 0] = whole[i][:HALF]
            own[2 * p + i, 1] = whole[i][HALF:]
        if p == 0:
            pl.semaphore_wait(barrier, len(AROUND) + NH - 1 + group)
        for dz, dx in AROUND:
            @pl.when(lax.div(near_by(dz, dx)[1], 2) == p)
            def _():
                x_copy(dz, dx).start()

    pair_states(0)
    for g in range(GROUPS - 1):
        @pl.when(group > g)
        def _():
            pl.semaphore_signal(ready.at[group - 1], 1, device_id=counterpart(g), device_id_type=MESH)
    q_copy.start()
    pair_states(1)
    xrecv[odd, x] = own[x, part]
    for copy in small:
        copy.wait()

    for h in range(HEADS_HERE):
        s = [leaf_state[j, h] for j in range(LEAVES)]
        sums = fenwick(s, weight(h, 1), weight(h, 2), weight(h, 3))
        local[0, h] = jnp.zeros((HEAD_DIM, HEAD_DIM), jnp.bfloat16)
        for j in range(1, LEAVES):
            local[j, h] = sums[j].astype(jnp.bfloat16)

    causal = lax.broadcasted_iota(jnp.int32, (LEAF, LEAF), 1) <= lax.broadcasted_iota(jnp.int32, (LEAF, LEAF), 0)

    def near(j, _):
        rows = pl.ds(pl.multiple_of(j * LEAF, LEAF), LEAF)
        for h in range(HEADS_HERE):
            columns = slice(h * HEAD_DIM, (h + 1) * HEAD_DIM)
            qs = q[rows, columns]
            scores = dot(qs, kv[0, rows, columns], NT)
            rounded = jnp.where(causal, scores * weight(h, 0), 0.0).astype(jnp.bfloat16)
            comb[h, rows] = dot(rounded, kv[1, rows, columns]) + dot(qs, local[j, h])
        return 0

    q_copy.wait()
    lax.fori_loop(0, 3, near, 0)

    def all_but_one(ref, sem):
        seven = ref.at[pl.ds(0, len(AROUND))]
        return pltpu.make_async_copy(seven, seven, sem)

    all_but_one(xrecv.reshape(2 * NX, HALF, HEAD_DIM), x_recv).wait()
    row = [[xrecv[i, j] for j in range(NX)] for i in range(2)]
    row_sum = [(r[0] + r[1]) + (r[2] + r[3]) for r in row]
    total[...] = row_sum[0] + row_sum[1]
    for g in range(GROUPS - 1, 0, -1):
        @pl.when(group < g)
        def _():
            pl.semaphore_wait(ready.at[g - 1], 1)
            t_copy(g).start()

    reached = jnp.where(group == GROUPS - 1, 4, 3)
    lax.fori_loop(3, reached, near, 0)

    for g in range(GROUPS - 1):
        @pl.when(group > g)
        def _():
            pltpu.make_async_copy(earlier.at[g], earlier.at[g], t_recv.at[g]).wait()
    far_weight = jnp.where(group >= 2, weight(x, 8), 0.0)
    base = (
        (far_weight + jnp.where(group == 1, weight(x, 7), 0.0)) * earlier[0]
        + far_weight * earlier[1]
        + jnp.where(group == 3, weight(x, 7), 0.0) * earlier[2])
    for i in range(2):
        sums = fenwick(row[i], weight(x, 4), weight(x, 5))
        if i:
            base = base + weight(x, 6) * row_sum[0]
        dsend[i, 0] = base
        for j in range(1, NX):
            dsend[i, j] = base + sums[j]
    for dz, dx in AROUND:
        d_copy(dz, dx).start()
    far[x, part] = dsend[odd, x]

    lax.fori_loop(reached, LEAVES, near, 0)

    def s_copy(c, d):
        return pltpu.make_async_remote_copy(
            ssq.at[c], ssq_in.at[c, d - 1], s_send.at[c], s_recv.at[c],
            device_id={"head": lax.rem(head + d, NH)}, device_id_type=MESH)

    ones = jnp.ones((8, 2 * HEAD_DIM), jnp.bfloat16)
    order = (0, 1, 3, 2)
    for dx in order:
        h = lax.rem(x + NX - dx, NX)
        arrived = far.at[h] if dx else far.at[h, part]
        pltpu.make_async_copy(arrived, arrived, d_recv.at[dx]).wait()
        state = jnp.concatenate([far[h, 0], far[h, 1]], axis=0)
        state = state.astype(jnp.bfloat16)
        columns = pl.ds(pl.multiple_of(h * HEAD_DIM, HEAD_DIM), HEAD_DIM)
        for j in range(LEAVES):
            rows = slice(j * LEAF, (j + 1) * LEAF)
            if j % 4 == 0:
                qs = q[j * LEAF:(j + 4) * LEAF, columns]
                both = dot(qs, state)
            value = comb[h, rows] + both[j % 4 * LEAF:(j % 4 + 1) * LEAF]
            comb[h, rows] = value
            squares = value * value
            if dx != order[0]:
                squares = squares + square_sum[rows]
            if dx != order[-1]:
                square_sum[rows] = squares
                continue
            top = squares.astype(jnp.bfloat16)
            rest = (squares - top.astype(jnp.float32)).astype(jnp.bfloat16)
            line = dot(ones, jnp.concatenate([top, rest], axis=1), NT)
            c, i = divmod(j, LEAVES // CHUNKS)
            ssq[c, 2 * i:2 * i + 1] = line[:1, :HEAD_DIM]
            ssq[c, 2 * i + 1:2 * i + 2] = line[:1, HEAD_DIM:]
            if i == LEAVES // CHUNKS - 1:
                for d in range(1, NH):
                    s_copy(c, d).start()

    for c in range(CHUNKS):
        pltpu.make_async_copy(ssq_in.at[c], ssq_in.at[c], s_recv.at[c]).wait()
        a = [ssq[c]] + [ssq_in[c, d] for d in range(NH - 1)]
        whole = ((a[0] + a[1]) + (a[2] + a[3])) + ((a[4] + a[5]) + (a[6] + a[7]))
        inverse = lax.rsqrt(whole * (1.0 / D) + EPSILON).T
        for i in range(ROWS // HEAD_DIM):
            rows = slice(c * ROWS + i * HEAD_DIM, c * ROWS + (i + 1) * HEAD_DIM)
            for h in range(HEADS_HERE):
                columns = slice(h * HEAD_DIM, (h + 1) * HEAD_DIM)
                out_ref[rows, columns] = (
                    comb[h, rows] * inverse[:, i:i + 1] * gain[:, columns]).astype(jnp.bfloat16)

    all_but_one(own.reshape(2 * NX, HALF, HEAD_DIM), x_send).wait()
    all_but_one(dsend.reshape(2 * NX, HALF, HEAD_DIM), d_send).wait()
    for g in range(1, GROUPS):
        @pl.when(group < g)
        def _():
            t_copy(g).wait_send()
    for c in range(CHUNKS):
        pltpu.make_async_copy(ssq_in.at[c], ssq_in.at[c], s_send.at[c]).wait()


def shards(queries, keys, values, level_table, head_table, gain):
    f32, bf16 = jnp.float32, jnp.bfloat16
    dma = pltpu.SemaphoreType.DMA
    square, half = (HEAD_DIM, HEAD_DIM), (HALF, HEAD_DIM)
    anywhere = pl.BlockSpec(memory_space=pltpu.HBM)
    vmem = pl.BlockSpec(memory_space=pltpu.VMEM)
    return pl.pallas_call(
        kernel,
        out_shape=pltpu.VMEM((SEG, WIDTH), bf16),
        in_specs=[anywhere] * 6,
        out_specs=vmem,
        scratch_shapes=[
            pltpu.SMEM(level_table.shape, f32),
            pltpu.SMEM(head_table.shape, jnp.int32),
            pltpu.VMEM((1, WIDTH), f32),
            pltpu.VMEM((SEG, WIDTH), bf16),
            pltpu.VMEM((2, SEG, WIDTH), bf16),
            pltpu.VMEM((HEADS_HERE, SEG, HEAD_DIM), f32),
            pltpu.VMEM((SEG, HEAD_DIM), f32),
            pltpu.VMEM((LEAVES, HEADS_HERE, *square), f32),
            pltpu.VMEM((LEAVES, HEADS_HERE, *square), bf16),
            pltpu.VMEM((HEADS_HERE, 2, *half), f32),
            pltpu.VMEM((2, NX, *half), f32),
            pltpu.VMEM(half, f32),
            pltpu.VMEM((GROUPS - 1, *half), f32),
            pltpu.VMEM((2, NX, *half), f32),
            pltpu.VMEM((HEADS_HERE, 2, *half), f32),
            pltpu.VMEM((CHUNKS, ROWS // HEAD_DIM, HEAD_DIM), f32),
            pltpu.VMEM((CHUNKS, NH - 1, ROWS // HEAD_DIM, HEAD_DIM), f32),
            dma((3,)), dma((HEADS_HERE // 2, SEG // CHUNK)), dma,
            dma, dma,
            dma((GROUPS - 1,)), dma((GROUPS - 1,)),
            dma, dma((NX,)),
            dma((CHUNKS,)), dma((CHUNKS,)),
            pltpu.SemaphoreType.REGULAR((GROUPS - 1,)),
        ],
        compiler_params=pltpu.CompilerParams(
            collective_id=0, has_side_effects=True, vmem_limit_bytes=40 * 1024 * 1024),
        name="attend",
    )(*[pltpu.with_memory_space_constraint(a, pltpu.HBM) for a in
       (queries, keys, values, level_table, head_table, gain.reshape(1, WIDTH))])


def solution(mesh):
    return jax.shard_map(
        shards,
        mesh=mesh,
        in_specs=(P("ctx", "head"), P("ctx", "head"), P("ctx", "head"), P(), P(), P("head")),
        out_specs=P("ctx", "head"),
        check_vma=False,
    )
```

time: 29.9 us -> 26.8 us (0.90)
  the two profiles are of different devices: /device:TPU:1 before, /device:TPU:225 now
where the time goes in v3:
time: 26.8 us; the launch traced here: 26.5 us
  Pallas kernels  25.2 us (94%)
  local copies, waits for them, and re-layouts  1.32 us (5%)
    pallas_call x1, Pallas kernels, shards(): pl.pallas_call(kernel, out_shape=pltpu.VMEM((SEG, WIDTH), bf16), in_specs...  25.2 us
    unnamed x1, local copies, waits for them, and re-layouts  1.32 us

profile of v3, /device:TPU:225, one launch (start us, length us, event | category | flops | bytes accessed | tf_op | source)
XLA Modules:
  0.0 26.5 jit_solution(6240717681716977896)
XLA Ops:
  0.0 25.2 %attend.1 = bf16[2048,512]{1,0:T(8,128)(2,1)S(1)} custom-call(bf16[2048,512]{1,0:T(8,128)(2,1)} %q_hbm.1, bf16[2048,512]{1,0:T(8,128)(2,1)} %k_hbm.1, bf16[2048,512]{1,0:T(8,128)(2,1)} %v_hbm.1, f32[4,9]{1,0:T(4,128)} %table_hbm.1, s32[32]{0:T(128)} %head_table_hbm.1, f32[1,512]{1,0:T(1,128)} %bitcast.1), custom_call_target="tpu_custom_call" | custom-call | tf_op jit(solution)/shard_map/attend/pallas_call | solution.py:282
  25.2 1.3 %copy.8 = bf16[2048,512]{1,0:T(8,128)(2,1)} copy(bf16[2048,512]{1,0:T(8,128)(2,1)S(1)} %attend.1) | data formatting | bytes 4194304

commit v4 on v3

--- a/solution.py
+++ b/solution.py
@@ -16,7 +16,7 @@
 SEG = LEAF * LEAVES
 WIDTH = HEADS_HERE * HEAD_DIM
 NX, GROUPS, NH = 4, 4, 8
-HALF = HEAD_DIM // 2
+STRIP = HEAD_DIM // 4
 PAIR = 2 * HEAD_DIM
 CHUNK = 2 * LEAF
 AROUND = [(1, 2), (1, 1), (1, 3), (0, 2), (1, 0), (0, 1), (0, 3)]
@@ -68,56 +68,60 @@
     def kv_part(p, c):
         return pl.ds(c * CHUNK, CHUNK), pl.ds(p * PAIR, PAIR)
 
-    for p in range(HEADS_HERE // 2):
+    def kv_start(p):
         for c in range(SEG // CHUNK):
             here = kv_part(p, c)
             pltpu.make_async_copy(k_hbm.at[here], kv.at[(0, *here)], kv_sem.at[p, c]).start()
             pltpu.make_async_copy(v_hbm.at[here], kv.at[(1, *here)], kv_sem.at[p, c]).start()
+
+    def near_by(dz, dx):
+        to_odd, to_x = lax.rem(odd + dz, 2), lax.rem(x + dx, NX)
+        return to_odd, to_x, {"ctx": (2 * group + to_odd) * NX + to_x}
+
+    def counterpart(g):
+        return {"ctx": (2 * g + lax.rem(part + g // 2, 2)) * NX + x}
+
+    barrier = pltpu.get_barrier_semaphore()
+    for dz, dx in AROUND:
+        pl.semaphore_signal(barrier, 1, device_id=near_by(dz, dx)[2], device_id_type=MESH)
+    kv_start(0)
+    for d in range(1, NH):
+        pl.semaphore_signal(barrier, 1, device_id={"head": lax.rem(head + d, NH)}, device_id_type=MESH)
+    for g in range(1, GROUPS):
+        @pl.when(group < g)
+        def _():
+            pl.semaphore_signal(barrier, 1, device_id=counterpart(g), device_id_type=MESH)
+    kv_start(1)
     small = [
         pltpu.make_async_copy(a, b, small_sem.at[i])
         for i, (a, b) in enumerate(((table_hbm, table), (head_table_hbm, head_table), (gain_hbm, gain)))]
     for copy in small:
         copy.start()
     q_copy = pltpu.make_async_copy(q_hbm, q, q_sem)
-
-    def near_by(dz, dx):
-        to_odd, to_x = lax.rem(odd + dz, 2), lax.rem(x + dx, NX)
-        return to_odd, to_x, {"ctx": (2 * group + to_odd) * NX + to_x}
-
-    def counterpart(g):
-        return {"ctx": (2 * g + lax.rem(part + g // 2, 2)) * NX + x}
-
     for g in range(GROUPS - 1):
-        earlier[g] = jnp.zeros((HALF, HEAD_DIM), jnp.float32)
-    barrier = pltpu.get_barrier_semaphore()
-    for dz, dx in AROUND:
-        pl.semaphore_signal(barrier, 1, device_id=near_by(dz, dx)[2], device_id_type=MESH)
-    for g in range(1, GROUPS):
-        @pl.when(group < g)
-        def _():
-            pl.semaphore_signal(barrier, 1, device_id=counterpart(g), device_id_type=MESH)
-    for d in range(1, NH):
-        pl.semaphore_signal(barrier, 1, device_id={"head": lax.rem(head + d, NH)}, device_id_type=MESH)
+        for p in range(HEADS_HERE // 2):
+            earlier[p, g] = jnp.zeros((STRIP, HEAD_DIM), jnp.float32)
 
     def weight(h, level):
         return table[head_table[head * HEADS_HERE + h], level] * SCALES[level]
 
-    def x_copy(dz, dx):
+    strip = 2 * x + part
+
+    def x_copy(p, dz, dx):
         to_odd, to_x, to = near_by(dz, dx)
         return pltpu.make_async_remote_copy(
-            own.at[to_x, lax.rem(to_odd + lax.div(z, 4), 2)], xrecv.at[odd, x],
-            x_send, x_recv, device_id=to, device_id_type=MESH)
-
-    def t_copy(g):
+            own.at[p, 2 * to_x + lax.rem(to_odd + lax.div(z, 4), 2)], xrecv.at[p, odd, x],
+            x_send, x_recv.at[p, odd], device_id=to, device_id_type=MESH)
+
+    def t_copy(p, g):
         return pltpu.make_async_remote_copy(
-            total, earlier.at[group], t_send.at[g - 1], t_recv.at[group],
+            total.at[p], earlier.at[p, group], t_send.at[p, g - 1], t_recv.at[p, group],
             device_id=counterpart(g), device_id_type=MESH)
 
-    def d_copy(dz, dx):
-        to_odd, to_x, to = near_by(dz, dx)
+    def d_copy(p, to_odd, to_x):
         return pltpu.make_async_remote_copy(
-            dsend.at[to_odd, to_x], far.at[x, part],
-            d_send, d_recv.at[dx], device_id=to, device_id_type=MESH)
+            dsend.at[p, to_odd, to_x], far.at[p, strip],
+            d_send, d_recv.at[p], device_id={"ctx": (2 * group + to_odd) * NX + to_x}, device_id_type=MESH)
 
     def pair_states(p):
         columns = slice(p * PAIR, (p + 1) * PAIR)
@@ -133,14 +137,13 @@
                     leaf_state[j, 2 * p + i] = two[i]
                 whole = two if whole is None else [m + n for m, n in zip(whole, two)]
         for i in range(2):
-            own[2 * p + i, 0] = whole[i][:HALF]
-            own[2 * p + i, 1] = whole[i][HALF:]
+            for r in range(4):
+                own[p, 4 * i + r] = whole[i][r * STRIP:(r + 1) * STRIP]
         if p == 0:
             pl.semaphore_wait(barrier, len(AROUND) + NH - 1 + group)
         for dz, dx in AROUND:
-            @pl.when(lax.div(near_by(dz, dx)[1], 2) == p)
-            def _():
-                x_copy(dz, dx).start()
+            x_copy(p, dz, dx).start()
+        pltpu.make_async_copy(own.at[p, strip], xrecv.at[p, odd, x], x_recv.at[p, odd]).start()
 
     pair_states(0)
     for g in range(GROUPS - 1):
@@ -149,7 +152,6 @@
             pl.semaphore_signal(ready.at[group - 1], 1, device_id=counterpart(g), device_id_type=MESH)
     q_copy.start()
     pair_states(1)
-    xrecv[odd, x] = own[x, part]
     for copy in small:
         copy.wait()
 
@@ -175,42 +177,78 @@
     q_copy.wait()
     lax.fori_loop(0, 3, near, 0)
 
-    def all_but_one(ref, sem):
-        seven = ref.at[pl.ds(0, len(AROUND))]
-        return pltpu.make_async_copy(seven, seven, sem)
-
-    all_but_one(xrecv.reshape(2 * NX, HALF, HEAD_DIM), x_recv).wait()
-    row = [[xrecv[i, j] for j in range(NX)] for i in range(2)]
-    row_sum = [(r[0] + r[1]) + (r[2] + r[3]) for r in row]
-    total[...] = row_sum[0] + row_sum[1]
-    for g in range(GROUPS - 1, 0, -1):
-        @pl.when(group < g)
-        def _():
-            pl.semaphore_wait(ready.at[g - 1], 1)
-            t_copy(g).start()
+    pairs = range(HEADS_HERE // 2)
+
+    def weigh(p, i, base):
+        h = 2 * p + lax.div(x, 2)
+        row = [xrecv[p, i, j] for j in range(NX)]
+        if i:
+            even = (xrecv[p, 0, 0] + xrecv[p, 0, 1]) + (xrecv[p, 0, 2] + xrecv[p, 0, 3])
+            base = base + weight(h, 6) * even
+        sums = fenwick(row, weight(h, 4), weight(h, 5))
+        dsend[p, i, 0] = base
+        for j in range(1, NX):
+            dsend[p, i, j] = base + sums[j]
+
+    def give_row(p, i):
+        for dx in (2, 1, 3):
+            d_copy(p, i, lax.rem(x + dx, NX)).start()
+        @pl.when(odd != i)
+        def _():
+            d_copy(p, i, x).start()
+
+    def give_back(p, i, base):
+        weigh(p, i, base)
+        give_row(p, i)
+
+    def keep(p):
+        pltpu.make_async_copy(dsend.at[p, odd, x], far.at[p, strip], d_recv.at[p]).start()
+
+    def row_arrives(p, i):
+        pltpu.make_async_copy(xrecv.at[p, i], xrecv.at[p, i], x_recv.at[p, i]).wait()
+
+    @pl.when(group == 0)
+    def _():
+        for p in pairs:
+            row_arrives(p, 0)
+            give_back(p, 0, jnp.zeros((STRIP, HEAD_DIM), jnp.float32))
+    for p in pairs:
+        @pl.when(group > 0)
+        def _():
+            row_arrives(p, 0)
+        row_arrives(p, 1)
+        total[p] = sum(xrecv[p, i, j] for i in range(2) for j in range(NX))
+        for g in range(GROUPS - 1, 0, -1):
+            @pl.when(group < g)
+            def _():
+                if p == 0:
+                    pl.semaphore_wait(ready.at[g - 1], 1)
+                t_copy(p, g).start()
 
     reached = jnp.where(group == GROUPS - 1, 4, 3)
     lax.fori_loop(3, reached, near, 0)
 
-    for g in range(GROUPS - 1):
-        @pl.when(group > g)
-        def _():
-            pltpu.make_async_copy(earlier.at[g], earlier.at[g], t_recv.at[g]).wait()
-    far_weight = jnp.where(group >= 2, weight(x, 8), 0.0)
-    base = (
-        (far_weight + jnp.where(group == 1, weight(x, 7), 0.0)) * earlier[0]
-        + far_weight * earlier[1]
-        + jnp.where(group == 3, weight(x, 7), 0.0) * earlier[2])
-    for i in range(2):
-        sums = fenwick(row[i], weight(x, 4), weight(x, 5))
-        if i:
-            base = base + weight(x, 6) * row_sum[0]
-        dsend[i, 0] = base
-        for j in range(1, NX):
-            dsend[i, j] = base + sums[j]
-    for dz, dx in AROUND:
-        d_copy(dz, dx).start()
-    far[x, part] = dsend[odd, x]
+    for p in pairs:
+        for g in range(GROUPS - 1):
+            @pl.when(group > g)
+            def _():
+                pltpu.make_async_copy(earlier.at[p, g], earlier.at[p, g], t_recv.at[p, g]).wait()
+        h = 2 * p + lax.div(x, 2)
+        far_weight = jnp.where(group >= 2, weight(h, 8), 0.0)
+        base = (
+            (far_weight + jnp.where(group == 1, weight(h, 7), 0.0)) * earlier[p, 0]
+            + far_weight * earlier[p, 1]
+            + jnp.where(group == 3, weight(h, 7), 0.0) * earlier[p, 2])
+        @pl.when(group == 0)
+        def _():
+            give_back(p, 1, base)
+        @pl.when(group > 0)
+        def _():
+            weigh(p, 0, base)
+            weigh(p, 1, base)
+            for dz, dx in AROUND:
+                d_copy(p, lax.rem(odd + dz, 2), lax.rem(x + dx, NX)).start()
+        keep(p)
 
     lax.fori_loop(reached, LEAVES, near, 0)
 
@@ -220,25 +258,24 @@
             device_id={"head": lax.rem(head + d, NH)}, device_id_type=MESH)
 
     ones = jnp.ones((8, 2 * HEAD_DIM), jnp.bfloat16)
-    order = (0, 1, 3, 2)
-    for dx in order:
-        h = lax.rem(x + NX - dx, NX)
-        arrived = far.at[h] if dx else far.at[h, part]
-        pltpu.make_async_copy(arrived, arrived, d_recv.at[dx]).wait()
-        state = jnp.concatenate([far[h, 0], far[h, 1]], axis=0)
-        state = state.astype(jnp.bfloat16)
-        columns = pl.ds(pl.multiple_of(h * HEAD_DIM, HEAD_DIM), HEAD_DIM)
+    zero = jnp.zeros((HEAD_DIM, HEAD_DIM), jnp.bfloat16)
+    for p in pairs:
+        pltpu.make_async_copy(far.at[p], far.at[p], d_recv.at[p]).wait()
+        first, second = [
+            far[p, 4 * i:4 * i + 4].reshape(HEAD_DIM, HEAD_DIM).astype(jnp.bfloat16) for i in range(2)]
+        state = jnp.concatenate([
+            jnp.concatenate([first, zero], axis=1), jnp.concatenate([zero, second], axis=1)], axis=0)
         for j in range(LEAVES):
             rows = slice(j * LEAF, (j + 1) * LEAF)
             if j % 4 == 0:
-                qs = q[j * LEAF:(j + 4) * LEAF, columns]
-                both = dot(qs, state)
-            value = comb[h, rows] + both[j % 4 * LEAF:(j % 4 + 1) * LEAF]
-            comb[h, rows] = value
-            squares = value * value
-            if dx != order[0]:
-                squares = squares + square_sum[rows]
-            if dx != order[-1]:
+                both = dot(q[j * LEAF:(j + 4) * LEAF, p * PAIR:(p + 1) * PAIR], state)
+            squares = square_sum[rows] if p else None
+            for i in range(2):
+                value = comb[2 * p + i, rows] + both[
+                    j % 4 * LEAF:(j % 4 + 1) * LEAF, i * HEAD_DIM:(i + 1) * HEAD_DIM]
+                comb[2 * p + i, rows] = value
+                squares = value * value if squares is None else squares + value * value
+            if p == 0:
                 square_sum[rows] = squares
                 continue
             top = squares.astype(jnp.bfloat16)
@@ -263,12 +300,14 @@
                 out_ref[rows, columns] = (
                     comb[h, rows] * inverse[:, i:i + 1] * gain[:, columns]).astype(jnp.bfloat16)
 
-    all_but_one(own.reshape(2 * NX, HALF, HEAD_DIM), x_send).wait()
-    all_but_one(dsend.reshape(2 * NX, HALF, HEAD_DIM), d_send).wait()
-    for g in range(1, GROUPS):
-        @pl.when(group < g)
-        def _():
-            t_copy(g).wait_send()
+    for ref, sem in ((own, x_send), (dsend, d_send)):
+        sent = ref.reshape(4 * NX, STRIP, HEAD_DIM).at[pl.ds(0, 2 * len(AROUND))]
+        pltpu.make_async_copy(sent, sent, sem).wait()
+    for p in pairs:
+        for g in range(1, GROUPS):
+            @pl.when(group < g)
+            def _():
+                t_copy(p, g).wait_send()
     for c in range(CHUNKS):
         pltpu.make_async_copy(ssq_in.at[c], ssq_in.at[c], s_send.at[c]).wait()
 
@@ -276,7 +315,7 @@
 def shards(queries, keys, values, level_table, head_table, gain):
     f32, bf16 = jnp.float32, jnp.bfloat16
     dma = pltpu.SemaphoreType.DMA
-    square, half = (HEAD_DIM, HEAD_DIM), (HALF, HEAD_DIM)
+    square, strip = (HEAD_DIM, HEAD_DIM), (STRIP, HEAD_DIM)
     anywhere = pl.BlockSpec(memory_space=pltpu.HBM)
     vmem = pl.BlockSpec(memory_space=pltpu.VMEM)
     return pl.pallas_call(
@@ -294,18 +333,18 @@
             pltpu.VMEM((SEG, HEAD_DIM), f32),
             pltpu.VMEM((LEAVES, HEADS_HERE, *square), f32),
             pltpu.VMEM((LEAVES, HEADS_HERE, *square), bf16),
-            pltpu.VMEM((HEADS_HERE, 2, *half), f32),
-            pltpu.VMEM((2, NX, *half), f32),
-            pltpu.VMEM(half, f32),
-            pltpu.VMEM((GROUPS - 1, *half), f32),
-            pltpu.VMEM((2, NX, *half), f32),
-            pltpu.VMEM((HEADS_HERE, 2, *half), f32),
+            pltpu.VMEM((2, 8, *strip), f32),
+            pltpu.VMEM((2, 2, NX, *strip), f32),
+            pltpu.VMEM((2, *strip), f32),
+            pltpu.VMEM((2, GROUPS - 1, *strip), f32),
+            pltpu.VMEM((2, 2, NX, *strip), f32),
+            pltpu.VMEM((2, 8, *strip), f32),
             pltpu.VMEM((CHUNKS, ROWS // HEAD_DIM, HEAD_DIM), f32),
             pltpu.VMEM((CHUNKS, NH - 1, ROWS // HEAD_DIM, HEAD_DIM), f32),
             dma((3,)), dma((HEADS_HERE // 2, SEG // CHUNK)), dma,
-            dma, dma,
-            dma((GROUPS - 1,)), dma((GROUPS - 1,)),
-            dma, dma((NX,)),
+            dma, dma((2, 2)),
+            dma((2, GROUPS - 1)), dma((2, GROUPS - 1)),
+            dma, dma((2,)),
             dma((CHUNKS,)), dma((CHUNKS,)),
             pltpu.SemaphoreType.REGULAR((GROUPS - 1,)),
         ],

time: 26.8 us -> 25.1 us (0.937)
  Pallas kernels: 25.2 us -> 23.7 us
    pallas_call x1, Pallas kernels: 25.2 us -> 23.7 us  [shards(): pl.pallas_call(kernel, out_shape=pltpu.VMEM((SEG, WIDTH), bf16), in_specs...]
where the time goes in v4:
time: 25.1 us; the launch traced here: 25 us
  Pallas kernels  23.7 us (94%)
  local copies, waits for them, and re-layouts  1.32 us (5%)
    pallas_call x1, Pallas kernels, shards(): pl.pallas_call(kernel, out_shape=pltpu.VMEM((SEG, WIDTH), bf16), in_specs...  23.7 us
    unnamed x1, local copies, waits for them, and re-layouts  1.32 us

profile of v4, /device:TPU:225, one launch (start us, length us, event | category | flops | bytes accessed | tf_op | source)
XLA Modules:
  0.0 25.0 jit_solution(1181217345947956588)
XLA Ops:
  0.0 23.7 %attend.1 = bf16[2048,512]{1,0:T(8,128)(2,1)S(1)} custom-call(bf16[2048,512]{1,0:T(8,128)(2,1)} %q_hbm.1, bf16[2048,512]{1,0:T(8,128)(2,1)} %k_hbm.1, bf16[2048,512]{1,0:T(8,128)(2,1)} %v_hbm.1, f32[4,9]{1,0:T(4,128)} %table_hbm.1, s32[32]{0:T(128)} %head_table_hbm.1, f32[1,512]{1,0:T(1,128)} %bitcast.1), custom_call_target="tpu_custom_call" | custom-call | tf_op jit(solution)/shard_map/attend/pallas_call | solution.py:321
  23.7 1.3 %copy.8 = bf16[2048,512]{1,0:T(8,128)(2,1)} copy(bf16[2048,512]{1,0:T(8,128)(2,1)S(1)} %attend.1) | data formatting | bytes 4194304

commit v5 on v4

--- a/solution.py
+++ b/solution.py
@@ -18,7 +18,7 @@
 NX, GROUPS, NH = 4, 4, 8
 STRIP = HEAD_DIM // 4
 PAIR = 2 * HEAD_DIM
-CHUNK = 2 * LEAF
+CHUNK = 8 * LEAF
 AROUND = [(1, 2), (1, 1), (1, 3), (0, 2), (1, 0), (0, 1), (0, 3)]
 CHUNKS = 2
 ROWS = SEG // CHUNKS
@@ -154,6 +154,7 @@
     pair_states(1)
     for copy in small:
         copy.wait()
+    far_weights = [[weight(2 * p + lax.div(x, 2), level) for level in range(4, 9)] for p in range(HEADS_HERE // 2)]
 
     for h in range(HEADS_HERE):
         s = [leaf_state[j, h] for j in range(LEAVES)]
@@ -180,12 +181,11 @@
     pairs = range(HEADS_HERE // 2)
 
     def weigh(p, i, base):
-        h = 2 * p + lax.div(x, 2)
         row = [xrecv[p, i, j] for j in range(NX)]
         if i:
             even = (xrecv[p, 0, 0] + xrecv[p, 0, 1]) + (xrecv[p, 0, 2] + xrecv[p, 0, 3])
-            base = base + weight(h, 6) * even
-        sums = fenwick(row, weight(h, 4), weight(h, 5))
+            base = base + far_weights[p][2] * even
+        sums = fenwick(row, far_weights[p][0], far_weights[p][1])
         dsend[p, i, 0] = base
         for j in range(1, NX):
             dsend[p, i, j] = base + sums[j]
@@ -218,7 +218,7 @@
             row_arrives(p, 0)
         row_arrives(p, 1)
         total[p] = sum(xrecv[p, i, j] for i in range(2) for j in range(NX))
-        for g in range(GROUPS - 1, 0, -1):
+        for g in range(1, GROUPS):
             @pl.when(group < g)
             def _():
                 if p == 0:
@@ -233,12 +233,11 @@
             @pl.when(group > g)
             def _():
                 pltpu.make_async_copy(earlier.at[p, g], earlier.at[p, g], t_recv.at[p, g]).wait()
-        h = 2 * p + lax.div(x, 2)
-        far_weight = jnp.where(group >= 2, weight(h, 8), 0.0)
+        far_weight = jnp.where(group >= 2, far_weights[p][4], 0.0)
         base = (
-            (far_weight + jnp.where(group == 1, weight(h, 7), 0.0)) * earlier[p, 0]
+            (far_weight + jnp.where(group == 1, far_weights[p][3], 0.0)) * earlier[p, 0]
             + far_weight * earlier[p, 1]
-            + jnp.where(group == 3, weight(h, 7), 0.0) * earlier[p, 2])
+            + jnp.where(group == 3, far_weights[p][3], 0.0) * earlier[p, 2])
         @pl.when(group == 0)
         def _():
             give_back(p, 1, base)

time: 25.1 us -> 24.6 us (0.980)
  Pallas kernels: 23.7 us -> 23.2 us
    pallas_call x1, Pallas kernels: 23.7 us -> 23.2 us  [shards(): pl.pallas_call(kernel, out_shape=pltpu.VMEM((SEG, WIDTH), bf16), in_specs...]
where the time goes in v5:
time: 24.6 us; the launch traced here: 24.5 us
  Pallas kernels  23.2 us (94%)
  local copies, waits for them, and re-layouts  1.32 us (5%)
    pallas_call x1, Pallas kernels, shards(): pl.pallas_call(kernel, out_shape=pltpu.VMEM((SEG, WIDTH), bf16), in_specs...  23.2 us
    unnamed x1, local copies, waits for them, and re-layouts  1.32 us

profile of v5, /device:TPU:225, one launch (start us, length us, event | category | flops | bytes accessed | tf_op | source)
XLA Modules:
  0.0 24.5 jit_solution(2689430672102638428)
XLA Ops:
  0.0 23.2 %attend.1 = bf16[2048,512]{1,0:T(8,128)(2,1)S(1)} custom-call(bf16[2048,512]{1,0:T(8,128)(2,1)} %q_hbm.1, bf16[2048,512]{1,0:T(8,128)(2,1)} %k_hbm.1, bf16[2048,512]{1,0:T(8,128)(2,1)} %v_hbm.1, f32[4,9]{1,0:T(4,128)} %table_hbm.1, s32[32]{0:T(128)} %head_table_hbm.1, f32[1,512]{1,0:T(1,128)} %bitcast.1), custom_call_target="tpu_custom_call" | custom-call | tf_op jit(solution)/shard_map/attend/pallas_call | solution.py:320
  23.2 1.3 %copy.8 = bf16[2048,512]{1,0:T(8,128)(2,1)} copy(bf16[2048,512]{1,0:T(8,128)(2,1)S(1)} %attend.1) | data formatting | bytes 4194304

commit v6 on v5

--- a/solution.py
+++ b/solution.py
@@ -225,6 +225,12 @@
                     pl.semaphore_wait(ready.at[g - 1], 1)
                 t_copy(p, g).start()
 
+    @pl.when(group > 0)
+    def _():
+        for p in pairs:
+            for i in range(2):
+                weigh(p, i, jnp.zeros((STRIP, HEAD_DIM), jnp.float32))
+
     reached = jnp.where(group == GROUPS - 1, 4, 3)
     lax.fori_loop(3, reached, near, 0)
 
@@ -243,8 +249,7 @@
             give_back(p, 1, base)
         @pl.when(group > 0)
         def _():
-            weigh(p, 0, base)
-            weigh(p, 1, base)
+            dsend[p] = dsend[p] + base
             for dz, dx in AROUND:
                 d_copy(p, lax.rem(odd + dz, 2), lax.rem(x + dx, NX)).start()
         keep(p)

time: 24.6 us -> 24.6 us (level)
  no operation moved by 1% of the time
where the time goes in v6:
time: 24.6 us; the launch traced here: 24.5 us
  Pallas kernels  23.2 us (94%)
  local copies, waits for them, and re-layouts  1.32 us (5%)
    pallas_call x1, Pallas kernels, shards(): pl.pallas_call(kernel, out_shape=pltpu.VMEM((SEG, WIDTH), bf16), in_specs...  23.2 us
    unnamed x1, local copies, waits for them, and re-layouts  1.32 us

profile of v6, /device:TPU:225, one launch (start us, length us, event | category | flops | bytes accessed | tf_op | source)
XLA Modules:
  0.0 24.5 jit_solution(9224590211338958901)
XLA Ops:
  0.0 23.2 %attend.1 = bf16[2048,512]{1,0:T(8,128)(2,1)S(1)} custom-call(bf16[2048,512]{1,0:T(8,128)(2,1)} %q_hbm.1, bf16[2048,512]{1,0:T(8,128)(2,1)} %k_hbm.1, bf16[2048,512]{1,0:T(8,128)(2,1)} %v_hbm.1, f32[4,9]{1,0:T(4,128)} %table_hbm.1, s32[32]{0:T(128)} %head_table_hbm.1, f32[1,512]{1,0:T(1,128)} %bitcast.1), custom_call_target="tpu_custom_call" | custom-call | tf_op jit(solution)/shard_map/attend/pallas_call | solution.py:325
  23.2 1.3 %copy.8 = bf16[2048,512]{1,0:T(8,128)(2,1)} copy(bf16[2048,512]{1,0:T(8,128)(2,1)S(1)} %attend.1) | data formatting | bytes 4194304
